TPU v7x, 32 devices: a whole 2x2x4 slice. The times are simulated.
32 devices in a mesh: pipe: 4 (over y, x), dp: 8 (over z, core).
Axes of the slice: x: 2, y: 2, z: 4, core: 2. Of those that a mesh axis runs over, the one named last changes fastest.
Arguments:
- x_in: bfloat16 [16, 1024, 512], P('dp', 'pipe'), may hold values from -6 to 6
- lengths: int32 [16], P('dp'), may hold values from 256 to 1024, as said below
- cotangent: bfloat16 [16, 1024, 512], P('dp', 'pipe'), may hold values from -6 to 6
- norm_gain: float32 [2, 512], replicated, may hold values from 0.5 to 1.5
- lambda_re: float32 [2, 384], replicated, may hold values from -1 to -0.1
- lambda_im: float32 [2, 384], replicated, may hold values from -8 to 8
- log_step: float32 [2, 384], replicated, may hold values from -6.9 to -2.3
- b_weight: float32 [2, 512, 768], P(None, 'dp'), may hold values from -0.25 to 0.25
- c_weight: float32 [2, 512, 768], P(None, 'dp'), may hold values from -2 to 2
- skip_weight: float32 [2, 512], replicated, may hold values from -4 to 4
- glu_weight: float32 [2, 512, 512], P(None, 'dp'), may hold values from -0.25 to 0.25
- glu_bias: float32 [2, 512], replicated, may hold values from -3 to 3
Outputs:
- output: bfloat16 [16, 1024, 512], P('dp', 'pipe')
- x_grad: bfloat16 [16, 1024, 512], P('dp', 'pipe')
- gain_grad: float32 [2, 512], replicated
- lambda_re_grad: float32 [2, 384], replicated
- lambda_im_grad: float32 [2, 384], replicated
- log_step_grad: float32 [2, 384], replicated
- b_grad: float32 [2, 512, 768], P(None, 'dp')
- c_grad: float32 [2, 512, 768], P(None, 'dp')
- skip_grad: float32 [2, 512], replicated
- glu_weight_grad: float32 [2, 512, 512], P(None, 'dp')
- glu_bias_grad: float32 [2, 512], replicated
Inputs may be any that keep to these rules, and one draw needn't show every extreme that they name: `lengths`: every length is 1024 or 256, and some sequence has length 1024.
All inputs are finite; a program needn't handle non-finite values.
Results may differ from a plain program's by a relative error of at most 0.025.
Values may be sent and summed in bfloat16 or wider, within the bound.
A program may use at most 320 MiB of HBM per device.

v0:
```python
import math

import jax
import jax.numpy as jnp
from jax import lax
from jax.sharding import PartitionSpec as P

EPSILON = 1e-05


def as_sent(shard):
    return jax.tree.map(lambda a: a.astype(jnp.bfloat16) if a.dtype == jnp.float32 else a, shard)


def shifted(value, axis, steps):
    count = lax.axis_size(axis)
    first, last = (max(0, -steps), min(count, count - steps))
    return lax.ppermute(value, axis, [(source, source + steps) for source in range(first, last)])


def discretize(lambda_real, lambda_imag, log_steps):
    step_size = jnp.exp(log_steps)
    radius = jnp.exp(lambda_real * step_size)
    angle_turn = lambda_imag * step_size
    decay_real = radius * jnp.cos(angle_turn)
    decay_imag = radius * jnp.sin(angle_turn)
    modulus = lambda_real * lambda_real + lambda_imag * lambda_imag
    coef_real = ((decay_real - 1.0) * lambda_real + decay_imag * lambda_imag) / modulus
    coef_imag = (decay_imag * lambda_real - (decay_real - 1.0) * lambda_imag) / modulus
    return (decay_real, decay_imag, coef_real, coef_imag)


def compose(earlier, latter):
    mul_real, mul_imag, add_real, add_imag = earlier
    next_mul_real, next_mul_imag, next_add_real, next_add_imag = latter
    return (
        next_mul_real * mul_real - next_mul_imag * mul_imag,
        next_mul_real * mul_imag + next_mul_imag * mul_real,
        next_mul_real * add_real - next_mul_imag * add_imag + next_add_real,
        next_mul_real * add_imag + next_mul_imag * add_real + next_add_imag,
    )


def in_order(values, reverse_flag):
    return jnp.where(reverse_flag, jnp.flip(values, 0), values)


def exact_gelu(values):
    return jax.nn.gelu(values, approximate=False)


def layer_norm(rows_wide, norm_gain, row_mask):
    average = jnp.mean(rows_wide, axis=1, keepdims=True)
    centred = rows_wide - average
    spread = jnp.mean(centred * centred, axis=1, keepdims=True)
    return centred * lax.rsqrt(spread + EPSILON) * norm_gain * row_mask[:, None]


def chained_scan(decay_real, decay_imag, drive_real, drive_imag):
    total_rows, width_state = drive_real.shape
    inner = math.gcd(16, total_rows)
    outer = total_rows // inner
    block_real = drive_real.reshape(outer, inner, width_state)
    block_imag = drive_imag.reshape(outer, inner, width_state)
    run_real = block_real[:, 0]
    run_imag = block_imag[:, 0]
    listed_real = [run_real]
    listed_imag = [run_imag]
    power_real = decay_real
    power_imag = decay_imag
    powers_real = [power_real]
    powers_imag = [power_imag]
    for offset in range(1, inner):
        next_real = decay_real * run_real - decay_imag * run_imag + block_real[:, offset]
        next_imag = decay_real * run_imag + decay_imag * run_real + block_imag[:, offset]
        run_real, run_imag = (next_real, next_imag)
        listed_real.append(run_real)
        listed_imag.append(run_imag)
        new_power_real = decay_real * power_real - decay_imag * power_imag
        new_power_imag = decay_real * power_imag + decay_imag * power_real
        power_real, power_imag = (new_power_real, new_power_imag)
        powers_real.append(power_real)
        powers_imag.append(power_imag)
    local_real = jnp.stack(listed_real, axis=1)
    local_imag = jnp.stack(listed_imag, axis=1)
    table_real = jnp.stack(powers_real, axis=0)
    table_imag = jnp.stack(powers_imag, axis=0)
    ends_real = local_real[:, -1]
    ends_imag = local_imag[:, -1]
    jump_real = jnp.broadcast_to(power_real, ends_real.shape)
    jump_imag = jnp.broadcast_to(power_imag, ends_real.shape)
    _, _, through_real, through_imag = lax.associative_scan(
        compose, (jump_real, jump_imag, ends_real, ends_imag)
    )
    zero_row = jnp.zeros((1, width_state), jnp.float32)
    carry_real = jnp.concatenate([zero_row, through_real[:-1]], axis=0)
    carry_imag = jnp.concatenate([zero_row, through_imag[:-1]], axis=0)
    full_real = (
        local_real + table_real[None] * carry_real[:, None] - table_imag[None] * carry_imag[:, None]
    )
    full_imag = (
        local_imag + table_real[None] * carry_imag[:, None] + table_imag[None] * carry_real[:, None]
    )
    return (full_real.reshape(total_rows, width_state), full_imag.reshape(total_rows, width_state))


def mixer_core(rows_in, row_mask, small_params, weights, reverse_flag):
    norm_gain, lambda_real, lambda_imag, log_steps, skip_gain, gate_bias = small_params
    proj_in, proj_out, gate_mat = weights
    normed = layer_norm(rows_in.astype(jnp.float32), norm_gain, row_mask).astype(jnp.bfloat16)
    coeffs = discretize(lambda_real, lambda_imag, log_steps)
    decay_real, decay_imag, coef_real, coef_imag = coeffs
    width_state = decay_real.shape[0]
    projected = jnp.dot(normed, proj_in, preferred_element_type=jnp.float32)
    proj_real = in_order(projected[:, :width_state], reverse_flag)
    proj_imag = in_order(projected[:, width_state:], reverse_flag)
    drive_real = coef_real * proj_real - coef_imag * proj_imag
    drive_imag = coef_real * proj_imag + coef_imag * proj_real
    scan_real, scan_imag = chained_scan(decay_real, decay_imag, drive_real, drive_imag)
    states = jnp.concatenate(
        [in_order(scan_real, reverse_flag), -in_order(scan_imag, reverse_flag)], axis=1
    ).astype(jnp.bfloat16)
    before = lax.dot_general(
        states, proj_out, (((1,), (1,)), ((), ())), preferred_element_type=jnp.float32
    )
    before = before + skip_gain * normed.astype(jnp.float32)
    return (normed, coeffs, proj_real, proj_imag, scan_real, scan_imag, states, before)


def spare_forward(rows_in, gated_in, row_mask, small_params, weights, reverse_flag):
    return (jnp.zeros_like(rows_in), jnp.zeros_like(rows_in))


def mixer_forward(rows_in, gated_in, row_mask, small_params, weights, reverse_flag):
    before = mixer_core(rows_in, row_mask, small_params, weights, reverse_flag)[-1]
    return (rows_in, exact_gelu(before).astype(jnp.bfloat16))


def glu_forward(rows_in, gated_in, row_mask, small_params, weights, reverse_flag):
    gate = jnp.dot(gated_in, weights[2], preferred_element_type=jnp.float32) + small_params[5]
    out_rows = rows_in.astype(jnp.float32) + row_mask[:, None] * (
        gated_in.astype(jnp.float32) * jax.nn.sigmoid(gate)
    )
    return (out_rows.astype(jnp.bfloat16), jnp.zeros_like(rows_in))


def empty_grads(rows_in, small_params, weights):
    zero_rows = jnp.zeros_like(rows_in)
    listing = [zero_rows, zero_rows]
    listing = listing + [jnp.zeros(matrix.shape, jnp.float32) for matrix in weights]
    return listing + [jnp.zeros_like(entry) for entry in small_params]


def spare_backward(
    rows_in, gated_in, row_mask, small_params, weights, reverse_flag, grad_rows, grad_gated
):
    return tuple(empty_grads(rows_in, small_params, weights))


def mixer_backward(
    rows_in, gated_in, row_mask, small_params, weights, reverse_flag, grad_rows, grad_gated
):
    norm_gain, lambda_real, lambda_imag, log_steps, skip_gain, gate_bias = small_params
    proj_in, proj_out, gate_mat = weights
    normed, coeffs, proj_real, proj_imag, scan_real, scan_imag, states, before = mixer_core(
        rows_in, row_mask, small_params, weights, reverse_flag
    )
    decay_real, decay_imag, coef_real, coef_imag = coeffs
    width_state = decay_real.shape[0]
    _, gelu_pull = jax.vjp(exact_gelu, before)
    grad_before = gelu_pull(grad_gated.astype(jnp.float32))[0].astype(jnp.bfloat16)
    grad_out_mat = lax.dot_general(
        grad_before, states, (((0,), (0,)), ((), ())), preferred_element_type=jnp.float32
    )
    grad_skip = jnp.sum(grad_before.astype(jnp.float32) * normed.astype(jnp.float32), axis=0)
    grad_states = jnp.dot(grad_before, proj_out, preferred_element_type=jnp.float32)
    back_real = jnp.flip(in_order(grad_states[:, :width_state], reverse_flag), 0)
    back_imag = jnp.flip(in_order(-grad_states[:, width_state:], reverse_flag), 0)
    adj_real, adj_imag = chained_scan(decay_real, -decay_imag, back_real, back_imag)
    adj_real = jnp.flip(adj_real, 0)
    adj_imag = jnp.flip(adj_imag, 0)
    zero_row = jnp.zeros((1, width_state), jnp.float32)
    prior_real = jnp.concatenate([zero_row, scan_real[:-1]], axis=0)
    prior_imag = jnp.concatenate([zero_row, scan_imag[:-1]], axis=0)
    grad_decay_real = jnp.sum(adj_real * prior_real + adj_imag * prior_imag, axis=0)
    grad_decay_imag = jnp.sum(adj_imag * prior_real - adj_real * prior_imag, axis=0)
    grad_coef_real = jnp.sum(adj_real * proj_real + adj_imag * proj_imag, axis=0)
    grad_coef_imag = jnp.sum(adj_imag * proj_real - adj_real * proj_imag, axis=0)
    grad_proj = jnp.concatenate(
        [
            in_order(coef_real * adj_real + coef_imag * adj_imag, reverse_flag),
            in_order(coef_real * adj_imag - coef_imag * adj_real, reverse_flag),
        ],
        axis=1,
    ).astype(jnp.bfloat16)
    grad_in_mat = lax.dot_general(
        normed, grad_proj, (((0,), (0,)), ((), ())), preferred_element_type=jnp.float32
    )
    grad_normed = lax.dot_general(
        grad_proj, proj_in, (((1,), (1,)), ((), ())), preferred_element_type=jnp.float32
    )
    grad_normed = grad_normed + skip_gain * grad_before.astype(jnp.float32)

    def norm_only(rows_wide, gain_wide):
        return layer_norm(rows_wide, gain_wide, row_mask)

    _, norm_pull = jax.vjp(norm_only, rows_in.astype(jnp.float32), norm_gain)
    grad_norm_rows, grad_gain = norm_pull(grad_normed)
    _, discrete_pull = jax.vjp(discretize, lambda_real, lambda_imag, log_steps)
    grad_lam_real, grad_lam_imag, grad_steps = discrete_pull(
        (grad_decay_real, grad_decay_imag, grad_coef_real, grad_coef_imag)
    )
    listing = empty_grads(rows_in, small_params, weights)
    listing[0] = (grad_norm_rows + grad_rows.astype(jnp.float32)).astype(jnp.bfloat16)
    listing[2] = grad_in_mat
    listing[3] = grad_out_mat
    listing[5] = grad_gain
    listing[6] = grad_lam_real
    listing[7] = grad_lam_imag
    listing[8] = grad_steps
    listing[9] = grad_skip
    return tuple(listing)


def glu_backward(
    rows_in, gated_in, row_mask, small_params, weights, reverse_flag, grad_rows, grad_gated
):
    gate_mat = weights[2]
    gate = jnp.dot(gated_in, gate_mat, preferred_element_type=jnp.float32) + small_params[5]
    sigmoid_gate = jax.nn.sigmoid(gate)
    grad_branch = row_mask[:, None] * grad_rows.astype(jnp.float32)
    grad_gate = (
        grad_branch * gated_in.astype(jnp.float32) * sigmoid_gate * (1.0 - sigmoid_gate)
    ).astype(jnp.bfloat16)
    grad_bias = jnp.sum(grad_gate.astype(jnp.float32), axis=0)
    grad_gate_mat = lax.dot_general(
        gated_in, grad_gate, (((0,), (0,)), ((), ())), preferred_element_type=jnp.float32
    )
    grad_act = grad_branch * sigmoid_gate + lax.dot_general(
        grad_gate, gate_mat, (((1,), (1,)), ((), ())), preferred_element_type=jnp.float32
    )
    listing = empty_grads(rows_in, small_params, weights)
    listing[0] = grad_rows
    listing[1] = grad_act.astype(jnp.bfloat16)
    listing[4] = grad_gate_mat
    listing[10] = grad_bias
    return tuple(listing)


def store(buffer, value, position, live):
    previous = lax.dynamic_index_in_dim(buffer, position, 0, keepdims=False)
    return lax.dynamic_update_index_in_dim(buffer, jnp.where(live, value, previous), position, 0)


def per_device(
    x_in,
    lengths,
    cotangent,
    norm_gain,
    lambda_re,
    lambda_im,
    log_step,
    b_weight,
    c_weight,
    skip_weight,
    glu_weight,
    glu_bias,
):
    section_index = lax.axis_index("pipe")
    depth = lax.axis_size("pipe")
    layer_index = section_index // 2
    gate_section = section_index % 2
    reverse_flag = layer_index == 1
    whole_x, whole_grad = (
        lax.all_gather(x_in, "pipe", axis=1, tiled=True),
        lax.all_gather(cotangent, "pipe", axis=1, tiled=True),
    )
    micro, length, model = whole_x.shape
    positions = jnp.arange(length, dtype=jnp.int32)
    row_masks = (positions[None, :] < lengths[:, None]).astype(jnp.float32)

    def pick(table):
        return lax.dynamic_index_in_dim(table, layer_index, 0, keepdims=False)

    small_params = (
        pick(norm_gain),
        pick(lambda_re),
        pick(lambda_im),
        pick(log_step),
        pick(skip_weight),
        pick(glu_bias),
    )
    shards = (
        pick(b_weight).astype(jnp.bfloat16),
        pick(c_weight).astype(jnp.bfloat16),
        pick(glu_weight).astype(jnp.bfloat16),
    )

    def weights_now():
        return (
            lax.all_gather(shards[0], "dp", axis=0, tiled=True),
            lax.all_gather(shards[1], "dp", axis=0, tiled=True),
            lax.all_gather(shards[2], "dp", axis=0, tiled=True),
        )

    zero_rows = jnp.zeros((length, model), jnp.bfloat16)
    stash_rows = jnp.zeros((micro, length, model), jnp.bfloat16)
    stash_gated = jnp.zeros((micro, length, model), jnp.bfloat16)
    results = jnp.zeros((micro, length, model), jnp.bfloat16)
    grad_inputs = jnp.zeros((micro, length, model), jnp.bfloat16)
    ticks = micro + depth - 1
    received = (zero_rows, zero_rows)
    for tick_number in range(ticks):
        slot = tick_number - section_index
        live = (slot >= 0) & (slot < micro)
        position = jnp.clip(slot, 0, micro - 1)
        row_mask = lax.dynamic_index_in_dim(row_masks, position, 0, keepdims=False)
        entering = lax.dynamic_index_in_dim(whole_x, position, 0, keepdims=False)
        rows_in = jnp.where(section_index == 0, entering, received[0])
        gated_in = received[1]
        weights = weights_now()
        branch = jnp.where(live, 1 + gate_section, 0)
        made = lax.switch(
            branch,
            (spare_forward, mixer_forward, glu_forward),
            rows_in,
            gated_in,
            row_mask,
            small_params,
            weights,
            reverse_flag,
        )
        stash_rows = store(stash_rows, rows_in, position, live)
        stash_gated = store(stash_gated, gated_in, position, live)
        results = store(results, made[0], position, live)
        if tick_number + 1 < ticks:
            received = shifted((as_sent(made[0]), as_sent(made[1])), "pipe", 1)
    local_rows = b_weight.shape[1]
    big_sums = (
        jnp.zeros((local_rows, b_weight.shape[2]), jnp.float32),
        jnp.zeros((local_rows, c_weight.shape[2]), jnp.float32),
        jnp.zeros((local_rows, glu_weight.shape[2]), jnp.float32),
    )
    small_sums = tuple((jnp.zeros_like(entry) for entry in small_params))
    received = (zero_rows, zero_rows)
    for tick_number in range(ticks):
        slot = tick_number - (depth - 1 - section_index)
        live = (slot >= 0) & (slot < micro)
        position = jnp.clip(slot, 0, micro - 1)
        row_mask = lax.dynamic_index_in_dim(row_masks, position, 0, keepdims=False)
        rows_in = lax.dynamic_index_in_dim(stash_rows, position, 0, keepdims=False)
        gated_in = lax.dynamic_index_in_dim(stash_gated, position, 0, keepdims=False)
        upstream = lax.dynamic_index_in_dim(whole_grad, position, 0, keepdims=False)
        grad_rows = jnp.where(section_index == depth - 1, upstream, received[0])
        grad_gated = received[1]
        weights = weights_now()
        branch = jnp.where(live, 1 + gate_section, 0)
        made = lax.switch(
            branch,
            (spare_backward, mixer_backward, glu_backward),
            rows_in,
            gated_in,
            row_mask,
            small_params,
            weights,
            reverse_flag,
            grad_rows,
            grad_gated,
        )
        reduced = (
            lax.psum_scatter(made[2], "dp", scatter_dimension=0, tiled=True),
            lax.psum_scatter(made[3], "dp", scatter_dimension=0, tiled=True),
            lax.psum_scatter(made[4], "dp", scatter_dimension=0, tiled=True),
        )
        big_sums = tuple((running + addend for running, addend in zip(big_sums, reduced)))
        small_sums = tuple((running + addend for running, addend in zip(small_sums, made[5:])))
        grad_inputs = store(grad_inputs, made[0], position, live)
        if tick_number + 1 < ticks:
            received = shifted((as_sent(made[0]), as_sent(made[1])), "pipe", -1)
    layer_count = norm_gain.shape[0]
    slot_weight = (jnp.arange(layer_count) == layer_index).astype(jnp.float32)

    def spread_layer(values):
        return slot_weight.reshape((layer_count,) + (1,) * values.ndim) * values[None]

    tables = tuple((spread_layer(entry) for entry in big_sums))
    small_stack = tuple((spread_layer(entry) for entry in small_sums))
    leaving = (
        lax.all_to_all(results[None], "pipe", split_axis=2, concat_axis=0, tiled=True),
        lax.all_to_all(grad_inputs[None], "pipe", split_axis=2, concat_axis=0, tiled=True),
    )
    output = leaving[0][depth - 1]
    x_grad = leaving[1][0]
    big_tables = (
        lax.psum(tables[0].astype(jnp.bfloat16), "pipe").astype(jnp.float32),
        lax.psum(tables[1].astype(jnp.bfloat16), "pipe").astype(jnp.float32),
        lax.psum(tables[2].astype(jnp.bfloat16), "pipe").astype(jnp.float32),
    )
    small_tables = lax.psum(
        (
            small_stack[0],
            small_stack[1],
            small_stack[2],
            small_stack[3],
            small_stack[4],
            small_stack[5],
        ),
        ("pipe", "dp"),
    )
    return (
        output,
        x_grad,
        small_tables[0],
        small_tables[1],
        small_tables[2],
        small_tables[3],
        big_tables[0],
        big_tables[1],
        small_tables[4],
        big_tables[2],
        small_tables[5],
    )


def solution(mesh):
    return jax.shard_map(
        per_device,
        mesh=mesh,
        in_specs=(
            P("dp", "pipe", None),
            P("dp"),
            P("dp", "pipe", None),
            P(),
            P(),
            P(),
            P(),
            P(None, "dp", None),
            P(None, "dp", None),
            P(),
            P(None, "dp", None),
            P(),
        ),
        out_specs=(
            P("dp", "pipe", None),
            P("dp", "pipe", None),
            P(),
            P(),
            P(),
            P(),
            P(None, "dp", None),
            P(None, "dp", None),
            P(),
            P(None, "dp", None),
            P(),
        ),
        check_vma=False,
    )
```

profile of v0, /device:TPU:0, one launch (start us, length us, event | category | flops | bytes accessed | tf_op | source)
XLA Modules:
  0.0 2912.9 jit_solution(13574490517839302923)
XLA Ops:
  15.4 16.5 all-gather.2
  31.8 15.6 all-gather.1
  47.5 17.4 all-gather
  67.1 194.6 %conditional.10 = (bf16[1024,512]{1,0:T(8,128)(2,1)}, bf16[1024,512]{1,0:T(8,128)(2,1)}) conditional(s32[]{:T(128)} %clamp.30, () %tuple.147, (pred[]{:T(512)}, f32[384]{0:T(512)S(1)}, f32[384]{0:T(512)S(1)}, f32[384]{0:T(512)S(1)}, bf16[1024,512]{1,0:T(8,128)(2,1)S(1)}, /*index=5*/f32[512]{0:T(512)S(1)}, f32[1024]{0:T(1024)S(1)}, ...), branch_computations={%region_0.1_spmd, %region_1.4_spmd, %region_4.5_spmd} | conditional | flops 1674205952 | bytes 143524400 | solution.py:323
  266.5 28.1 collective-permute-done
  295.1 30.8 %collective-permute-done.1 = bf16[1024,512]{1,0:T(8,128)(2,1)} collective-permute-done((bf16[1024,512]{1,0:T(8,128)(2,1)}, bf16[1024,512]{1,0:T(8,128)(2,1)}, u32[]{:S(2)}, u32[]{:S(2)}) %collective-permute-start.1) | collective-permute-done | bytes 1048608 | tf_op jit(solution)/shard_map/ppermute | solution.py:18
  325.9 195.1 %conditional.11 = (bf16[1024,512]{1,0:T(8,128)(2,1)}, bf16[1024,512]{1,0:T(8,128)(2,1)}) conditional(s32[]{:T(128)} %clamp.31, () %tuple.150, (pred[]{:T(512)}, f32[384]{0:T(512)S(1)}, f32[384]{0:T(512)S(1)}, f32[384]{0:T(512)S(1)}, bf16[1024,512]{1,0:T(8,128)(2,1)S(1)}, /*index=5*/f32[512]{0:T(512)S(1)}, f32[1024]{0:T(1024)}, ...), branch_computations={%region_5.6_spmd, %region_6.9_spmd, %region_9.10_spmd} | conditional | flops 1674205952 | bytes 143491536 | solution.py:323
  525.6 20.5 collective-permute-done.2
  546.6 21.1 collective-permute-done.3
  603.5 20.1 collective-permute-done.5
  639.8 196.8 %collective-permute-start.7 = (bf16[1024,512]{1,0:T(8,128)(2,1)}, bf16[1024,512]{1,0:T(8,128)(2,1)S(1)}, u32[]{:S(2)}, u32[]{:S(2)}) collective-permute-start(bf16[1024,512]{1,0:T(8,128)(2,1)} %get-tuple-element.795), channel_id=1, source_target_pairs={{0,8},{8,16},{16,24},{1,9},{9,17},{17,25},{2,10},{10,18},{18,26},{... | collective-permute-start | bytes 3145736 | tf_op jit(solution)/shard_map/ppermute | solution.py:18
  843.4 14.0 collective-permute-done.7
  873.8 43.2 %collective-permute-done.9 = bf16[1024,512]{1,0:T(8,128)(2,1)} collective-permute-done((bf16[1024,512]{1,0:T(8,128)(2,1)}, bf16[1024,512]{1,0:T(8,128)(2,1)}, u32[]{:S(2)}, u32[]{:S(2)}) %collective-permute-start.9) | collective-permute-done | bytes 1048608 | tf_op jit(solution)/shard_map/ppermute | solution.py:18
  919.7 16.5 collective-permute-done.8
  950.9 27.0 collective-permute-done.11
  980.5 15.8 collective-permute-done.10
  1011.5 575.7 %collective-permute-done.13 = bf16[1024,512]{1,0:T(8,128)(2,1)} collective-permute-done((bf16[1024,512]{1,0:T(8,128)(2,1)}, bf16[1024,512]{1,0:T(8,128)(2,1)}, u32[]{:S(2)}, u32[]{:S(2)}) %collective-permute-start.13) | collective-permute-done | bytes 1048608 | tf_op jit(solution)/shard_map/ppermute | solution.py:18
  1589.8 15.4 collective-permute-done.12
  1605.2 550.1 %conditional.18 = (bf16[1024,512]{1,0:T(8,128)(2,1)}, bf16[1024,512]{1,0:T(8,128)(2,1)}, f32[512,768]{1,0:T(8,128)}, f32[512,768]{1,0:T(8,128)}, f32[512,512]{1,...) conditional(s32[]{:T(128)} %clamp.38, () %tuple.170, ...), branch_computations={%region_65.66_spmd, %region_66.77_spmd, %region_77.79_spmd} | conditional | flops 4949612544 | bytes 333270720 | solution.py:358
  2157.9 27.0 collective-permute-done.15
  2187.6 14.5 collective-permute-done.14
  2202.1 542.7 %conditional.19 = (bf16[1024,512]{1,0:T(8,128)(2,1)S(1)}, f32[512,768]{1,0:T(8,128)}, f32[512,768]{1,0:T(8,128)}, f32[512,512]{1,0:T(8,128)S(1)}, f32[512]{0:T(5...) conditional(s32[]{:T(128)} %clamp.39, () %tuple.173, ...), branch_computations={%region_79.80_spmd, %region_80.91_spmd, %region_91.93_spmd} | conditional | flops 4949612544 | bytes 326307008 | solution.py:358
  2818.1 34.4 %reduce-scatter.6.cloned.1.call-done = f32[64,768]{1,0:T(8,128)} async-done(((f32[512,768]{1,0:T(8,128)}), f32[64,768]{1,0:T(8,128)}) %reduce-scatter.6.cloned.1.call-update) | async-done | bytes 196624 | tf_op jit(solution)/shard_map/reduce_scatter | solution.py:372
  2854.6 38.3 %all-reduce.374 = (f32[2,512]{1,0:T(2,128)}, f32[2,384]{1,0:T(2,128)}, f32[2,384]{1,0:T(2,128)}, f32[2,384]{1,0:T(2,128)}, f32[2,512]{1,0:T(2,128)}, /*index=5*/f32[2,512]{1,0:T(2,128)}) all-reduce(f32[2,512]{1,0:T(2,128)S(1)} %get-tuple-element.3562, ...), channel_id=1, replica_groups=mesh['pipe'=4,'dp'=8] {'pipe','dp'}, use_global_device_ids=true, to_apply=%region_93.94 | all-reduce | flops 5376 | bytes 43008 | tf_op jit(solution)/shard_map/psum | solution.py:399
  (2050 shorter events, 1718.6 us)
Async XLA Ops:
  7.2 57.7 %all-gather.6.cloned.1.call-start = ((), (), s32[]{:S(2)}) async-start(), calls=%async_computation.5 | async-start | bytes 2621440 | tf_op jit(solution)/shard_map/all_gather | solution.py:275
  7.9 584.9 %all-gather.8.cloned.1.call-start = ((), (), s32[]{:S(2)}) async-start(), calls=%async_computation.6 | async-start | bytes 2621440 | tf_op jit(solution)/shard_map/all_gather | solution.py:276
  261.8 32.8 %collective-permute-start = (bf16[1024,512]{1,0:T(8,128)(2,1)}, bf16[1024,512]{1,0:T(8,128)(2,1)}, u32[]{:S(2)}, u32[]{:S(2)}) collective-permute-start(bf16[1024,512]{1,0:T(8,128)(2,1)} %get-tuple-element.788), channel_id=1, source_target_pairs={{0,8},{8,16},{16,24},{1,9},{9,17},{17,25},{2,10},{10,18},{18,26},{... | collective-permute-start | bytes 3145736 | tf_op jit(solution)/shard_map/ppermute | solution.py:18
  264.1 2543.6 %reduce-scatter.8.cloned.1.call-start = ((), (), s32[]{:S(2)}) async-start(), calls=%async_computation.9 | async-start | bytes 1179648 | tf_op jit(solution)/shard_map/reduce_scatter | solution.py:373
  264.1 61.8 %collective-permute-start.1 = (bf16[1024,512]{1,0:T(8,128)(2,1)}, bf16[1024,512]{1,0:T(8,128)(2,1)}, u32[]{:S(2)}, u32[]{:S(2)}) collective-permute-start(bf16[1024,512]{1,0:T(8,128)(2,1)} %get-tuple-element.789), channel_id=1, source_target_pairs={{0,8},{8,16},{16,24},{1,9},{9,17},{17,25},{2,10},{10,18},{18,26},{... | collective-permute-start | bytes 3145736 | tf_op jit(solution)/shard_map/ppermute | solution.py:18
  521.0 25.1 collective-permute-start.2
  523.3 44.4 %collective-permute-start.3 = (bf16[1024,512]{1,0:T(8,128)(2,1)}, bf16[1024,512]{1,0:T(8,128)(2,1)}, u32[]{:S(2)}, u32[]{:S(2)}) collective-permute-start(bf16[1024,512]{1,0:T(8,128)(2,1)} %get-tuple-element.791), channel_id=1, source_target_pairs={{0,8},{8,16},{16,24},{1,9},{9,17},{17,25},{2,10},{10,18},{18,26},{... | collective-permute-start | bytes 3145736 | tf_op jit(solution)/shard_map/ppermute | solution.py:18
  573.9 29.1 collective-permute-start.4
  580.0 43.6 %collective-permute-start.5 = (bf16[1024,512]{1,0:T(8,128)(2,1)}, bf16[1024,512]{1,0:T(8,128)(2,1)}, u32[]{:S(2)}, u32[]{:S(2)}) collective-permute-start(bf16[1024,512]{1,0:T(8,128)(2,1)} %get-tuple-element.793), channel_id=1, source_target_pairs={{0,8},{8,16},{16,24},{1,9},{9,17},{17,25},{2,10},{10,18},{18,26},{... | collective-permute-start | bytes 3145736 | tf_op jit(solution)/shard_map/ppermute | solution.py:18
  630.3 211.5 %collective-permute-start.6 = (bf16[1024,512]{1,0:T(8,128)(2,1)}, bf16[1024,512]{1,0:T(8,128)(2,1)S(1)}, u32[]{:S(2)}, u32[]{:S(2)}) collective-permute-start(bf16[1024,512]{1,0:T(8,128)(2,1)} %get-tuple-element.794), channel_id=1, source_target_pairs={{0,8},{8,16},{16,24},{1,9},{9,17},{17,25},{2,10},{10,18},{18,26},{... | collective-permute-start | bytes 3145736 | tf_op jit(solution)/shard_map/ppermute | solution.py:18
  639.8 217.6 %collective-permute-start.7 = (bf16[1024,512]{1,0:T(8,128)(2,1)}, bf16[1024,512]{1,0:T(8,128)(2,1)S(1)}, u32[]{:S(2)}, u32[]{:S(2)}) collective-permute-start(bf16[1024,512]{1,0:T(8,128)(2,1)} %get-tuple-element.795), channel_id=1, source_target_pairs={{0,8},{8,16},{16,24},{1,9},{9,17},{17,25},{2,10},{10,18},{18,26},{... | collective-permute-start | bytes 3145736 | tf_op jit(solution)/shard_map/ppermute | solution.py:18
  871.2 45.8 %collective-permute-start.9 = (bf16[1024,512]{1,0:T(8,128)(2,1)}, bf16[1024,512]{1,0:T(8,128)(2,1)}, u32[]{:S(2)}, u32[]{:S(2)}) collective-permute-start(bf16[1024,512]{1,0:T(8,128)(2,1)} %get-tuple-element.796), channel_id=1, source_target_pairs={{8,0},{16,8},{24,16},{9,1},{17,9},{25,17},{10,2},{18,10},{26,18},{... | collective-permute-start | bytes 3145736 | tf_op jit(solution)/shard_map/ppermute | solution.py:18
  872.5 63.6 %collective-permute-start.8 = (bf16[1024,512]{1,0:T(8,128)(2,1)}, bf16[1024,512]{1,0:T(8,128)(2,1)}, u32[]{:S(2)}, u32[]{:S(2)}) collective-permute-start(bf16[1024,512]{1,0:T(8,128)(2,1)} %get-tuple-element.797), channel_id=1, source_target_pairs={{8,0},{16,8},{24,16},{9,1},{17,9},{25,17},{10,2},{18,10},{26,18},{... | collective-permute-start | bytes 3145736 | tf_op jit(solution)/shard_map/ppermute | solution.py:18
  948.3 29.6 %collective-permute-start.11 = (bf16[1024,512]{1,0:T(8,128)(2,1)}, bf16[1024,512]{1,0:T(8,128)(2,1)}, u32[]{:S(2)}, u32[]{:S(2)}) collective-permute-start(bf16[1024,512]{1,0:T(8,128)(2,1)} %get-tuple-element.798), channel_id=1, source_target_pairs={{8,0},{16,8},{24,16},{9,1},{17,9},{25,17},{10,2},{18,10},{26,18},{... | collective-permute-start | bytes 3145736 | tf_op jit(solution)/shard_map/ppermute | solution.py:18
  949.6 46.8 %collective-permute-start.10 = (bf16[1024,512]{1,0:T(8,128)(2,1)}, bf16[1024,512]{1,0:T(8,128)(2,1)}, u32[]{:S(2)}, u32[]{:S(2)}) collective-permute-start(bf16[1024,512]{1,0:T(8,128)(2,1)} %get-tuple-element.799), channel_id=1, source_target_pairs={{8,0},{16,8},{24,16},{9,1},{17,9},{25,17},{10,2},{18,10},{26,18},{... | collective-permute-start | bytes 3145736 | tf_op jit(solution)/shard_map/ppermute | solution.py:18
  1008.9 578.3 %collective-permute-start.13 = (bf16[1024,512]{1,0:T(8,128)(2,1)}, bf16[1024,512]{1,0:T(8,128)(2,1)}, u32[]{:S(2)}, u32[]{:S(2)}) collective-permute-start(bf16[1024,512]{1,0:T(8,128)(2,1)} %get-tuple-element.800), channel_id=1, source_target_pairs={{8,0},{16,8},{24,16},{9,1},{17,9},{25,17},{10,2},{18,10},{26,18},{... | collective-permute-start | bytes 3145736 | tf_op jit(solution)/shard_map/ppermute | solution.py:18
  1010.2 595.1 %collective-permute-start.12 = (bf16[1024,512]{1,0:T(8,128)(2,1)}, bf16[1024,512]{1,0:T(8,128)(2,1)}, u32[]{:S(2)}, u32[]{:S(2)}) collective-permute-start(bf16[1024,512]{1,0:T(8,128)(2,1)} %get-tuple-element.801), channel_id=1, source_target_pairs={{8,0},{16,8},{24,16},{9,1},{17,9},{25,17},{10,2},{18,10},{26,18},{... | collective-permute-start | bytes 3145736 | tf_op jit(solution)/shard_map/ppermute | solution.py:18
  2155.3 29.6 %collective-permute-start.15 = (bf16[1024,512]{1,0:T(8,128)(2,1)}, bf16[1024,512]{1,0:T(8,128)(2,1)}, u32[]{:S(2)}, u32[]{:S(2)}) collective-permute-start(bf16[1024,512]{1,0:T(8,128)(2,1)} %get-tuple-element.802), channel_id=1, source_target_pairs={{8,0},{16,8},{24,16},{9,1},{17,9},{25,17},{10,2},{18,10},{26,18},{... | collective-permute-start | bytes 3145736 | tf_op jit(solution)/shard_map/ppermute | solution.py:18
  2156.6 45.5 %collective-permute-start.14 = (bf16[1024,512]{1,0:T(8,128)(2,1)}, bf16[1024,512]{1,0:T(8,128)(2,1)}, u32[]{:S(2)}, u32[]{:S(2)}) collective-permute-start(bf16[1024,512]{1,0:T(8,128)(2,1)} %get-tuple-element.803), channel_id=1, source_target_pairs={{8,0},{16,8},{24,16},{9,1},{17,9},{25,17},{10,2},{18,10},{26,18},{... | collective-permute-start | bytes 3145736 | tf_op jit(solution)/shard_map/ppermute | solution.py:18
  2750.3 67.8 %reduce-scatter.4.cloned.1.call-start = ((), (), s32[]{:S(2)}) async-start(), calls=%async_computation.7 | async-start | bytes 1769472 | tf_op jit(solution)/shard_map/reduce_scatter | solution.py:371
  2768.0 24.6 all-to-all-start
  2772.5 80.1 %reduce-scatter.6.cloned.1.call-start = ((), (), s32[]{:S(2)}) async-start(), calls=%async_computation.8 | async-start | bytes 1769472 | tf_op jit(solution)/shard_map/reduce_scatter | solution.py:372
  2802.8 90.1 %all-to-all-start.1 = ((bf16[1,2,1024,512]{3,1,0,2:T(2,128)(2,1)}), bf16[1,2,1024,512]{3,1,0,2:T(2,128)(2,1)}, u32[]{:S(2)}, u32[]{:S(2)}) async-start(bf16[1,2,1024,512]{3,1,0,2:T(2,128)(2,1)} %copy.2704), calls=%async_computation.1 | async-start | bytes 4194304 | tf_op jit(solution)/shard_map/all_to_all | solution.py:390
  2807.2 93.6 %all-reduce.378.cloned.1.call-start = ((), (), s32[]{:S(2)}) async-start(), calls=%async_computation.10 | async-start | bytes 1048576 | tf_op jit(solution)/shard_map/psum | solution.py:395
  (403 other events, 5930.4 us)
Sparse Core Ops, SparseCore 0:
  9.9 38.0 all-gather.5
  264.2 48.7 all-gather.7
  2750.4 32.7 reduce-scatter.7
  2785.3 32.7 reduce-scatter.3
  2820.3 32.2 reduce-scatter.5
  2856.7 44.0 all-reduce.377
where the time goes:
time: 2970 us; the launch traced here: 2910 us
  local copies, waits for them, and re-layouts  1170 us (39%)
  waiting for transfers between devices  937 us (32%)
  other arithmetic  364 us (12%)
  starting transfers between devices  248 us (8%)
  blocking collectives  87.8 us (3%)
  matrix products  53.5 us (2%)
  loops' own time  41.1 us (1%)
    ppermute x16, waiting for transfers between devices, shifted(): lax.ppermute(value, axis, [(source, source + steps) for source in range(f...  875 us
    rev x24, local copies, waits for them, and re-layouts, in_order(): return jnp.where(reverse_flag, jnp.flip(values, 0), values)  298 us
    ppermute x16, starting transfers between devices, shifted(): lax.ppermute(value, axis, [(source, source + steps) for source in range(f...  239 us
    slice x222, local copies, waits for them, and re-layouts, chained_scan(): lax.associative_scan(compose, (jump_real, jump_imag, ends_real, ends_imag))  181 us
    pad x96, local copies, waits for them, and re-layouts, chained_scan(): lax.associative_scan(compose, (jump_real, jump_imag, ends_real, ends_imag))  116 us
    cond x726, local copies, waits for them, and re-layouts  74.6 us
    add x70, other arithmetic, chained_scan(): lax.associative_scan(compose, (jump_real, jump_imag, ends_real, ends_imag))  68.9 us
    add x56, local copies, waits for them, and re-layouts, chained_scan(): decay_real * run_real - decay_imag * run_imag + block_real[:, offset]  67 us
  transfers between devices with their start and end apart: 24, of which 19 were waited for; matrix products, arithmetic and copies ran while one was open for 9% of the time, Pallas kernels for 0%

commit v1 on v0

v1 whole, which is shorter than its diff:
```python
import functools

import jax
import jax.numpy as jnp
from jax import lax
from jax.experimental import pallas as pl
from jax.experimental.pallas import tpu as pltpu
from jax.sharding import PartitionSpec as P

EPSILON = 1e-05
CHUNKS = 8
TILE = 32
MESH = pl.DeviceIdType.MESH
F32 = jnp.float32
BF16 = jnp.bfloat16
NN = (((1,), (0,)), ((), ()))
NT = (((1,), (1,)), ((), ()))
TN = (((0,), (0,)), ((), ()))


def cmul(u, v):
    return (u[0] * v[0] - u[1] * v[1], u[0] * v[1] + u[1] * v[0])


def conj(u):
    return (u[0], -u[1])


def dot(a, b, dims):
    return lax.dot_general(a, b, dims, preferred_element_type=F32)


def discretize(lam_re, lam_im, log_step):
    step = jnp.exp(log_step)
    radius = jnp.exp(lam_re * step)
    turn = lam_im * step
    decay = (radius * jnp.cos(turn), radius * jnp.sin(turn))
    modulus = lam_re * lam_re + lam_im * lam_im
    coef = (
        ((decay[0] - 1.0) * lam_re + decay[1] * lam_im) / modulus,
        (decay[1] * lam_re - (decay[0] - 1.0) * lam_im) / modulus,
    )
    return step, decay, coef


def discretize_grads(lam_re, lam_im, log_step, decay_grad, coef_grad):
    step, decay, coef = discretize(lam_re, lam_im, log_step)
    lam = (lam_re, lam_im)
    modulus = lam_re * lam_re + lam_im * lam_im
    inverse = (lam_re / modulus, -lam_im / modulus)
    through = cmul(coef_grad, conj(inverse))
    total = (decay_grad[0] + through[0], decay_grad[1] + through[1])
    first = cmul(total, (step * decay[0], -step * decay[1]))
    second = cmul(coef_grad, conj(cmul(coef, inverse)))
    turned = cmul(total, conj(cmul(lam, decay)))
    return first[0] - second[0], first[1] - second[1], step * turned[0]


def main_kernel(
    depth,
    x_ref, cot_ref, len_ref, gain_ref, lre_ref, lim_ref, lst_ref, skip_ref, bias_ref, w_ref,
    out_ref, xg_ref, gpart_ref, small_ref,
    h_ref, go_ref, xhat_ref, rstd_ref, normed_ref, p_ref, z_ref, zb_ref, dg_ref, gated_ref, sig_ref,
    gg_ref, gb_ref, gp_ref, src_ref, tmp_ref, acc_ref,
    ends_ref, got_ref, send_sems, recv_sems,
):
    seqs, pos, model = x_ref.shape
    state = lre_ref.shape[1]
    layers = gain_ref.shape[0]
    rows = seqs * pos
    steps = pos // CHUNKS
    me, dp = lax.axis_index("pipe"), lax.axis_index("dp")

    def peer(k):
        return lax.rem(me + k, depth)

    barrier = pltpu.get_barrier_semaphore()
    for k in range(1, depth):
        pl.semaphore_signal(barrier, inc=1, device_id=(peer(k), dp), device_id_type=MESH)

    row = lax.broadcasted_iota(jnp.int32, (pos, pos), 0)
    col = lax.broadcasted_iota(jnp.int32, (pos, pos), 1)
    spread = (lax.rem(row, CHUNKS) * steps + lax.div(row, CHUNKS) == col).astype(F32).astype(BF16)
    masks = [(len_ref[q] > me * pos).astype(F32) for q in range(seqs)]
    sublane = lax.broadcasted_iota(jnp.int32, (CHUNKS, state), 0)

    def seq_rows(q):
        return pl.ds(q * pos, pos)

    def tiles(body, q, init=0, unroll=1):
        def step(i, carry):
            return body(pl.ds(pl.multiple_of(q * pos + i * TILE, TILE), TILE), masks[q], carry)
        return lax.fori_loop(0, pos // TILE, step, init, unroll=unroll)

    def all_tiles(body, init=0):
        for q in range(seqs):
            init = tiles(body, q, init)
        return init

    def fold(value):
        total = value[0:8]
        for r in range(8, value.shape[0], 8):
            total = total + value[r:r + 8]
        return total

    for q in range(seqs):
        h_ref[0, seq_rows(q), :] = dot(spread, x_ref[q], NN).astype(BF16)
        go_ref[seq_rows(q), :] = dot(spread, cot_ref[q], NN).astype(BF16)

    step_all, decay_all, coef_all = discretize(lre_ref[...], lim_ref[...], lst_ref[...])
    pl.semaphore_wait(barrier, depth - 1)

    def complex_rows(src, r):
        return (src[r, 0:state], src[r, state:2 * state])

    zero = jnp.zeros((CHUNKS, state), F32)

    def scan_ends(src, decay, down):
        def step(i, carry):
            s = (steps - 1 - i) if down else i
            made = []
            for q in range(seqs):
                r = pl.ds(pl.multiple_of(q * pos + s * CHUNKS, CHUNKS), CHUNKS)
                add = complex_rows(src, r)
                moved = cmul(decay, carry[q])
                made.append((moved[0] + add[0], moved[1] + add[1]))
            return tuple(made)
        return lax.fori_loop(0, steps, step, ((zero, zero),) * seqs, unroll=4)

    def shifted(value, k, down):
        rolled = pltpu.roll(value, CHUNKS - k if down else k, axis=0)
        keep = (sublane < CHUNKS - k) if down else (sublane >= k)
        return jnp.where(keep, rolled, 0.0)

    def squared(value, times):
        for _ in range(times):
            value = cmul(value, value)
        return value

    def start_exchange(number, ends, decay, down):
        power = squared(decay, steps.bit_length() - 1)
        jump, before = power, []
        sums = list(ends)
        k = 1
        while k < CHUNKS:
            for q in range(seqs):
                moved = cmul(jump, (shifted(sums[q][0], k, down), shifted(sums[q][1], k, down)))
                sums[q] = (sums[q][0] + moved[0], sums[q][1] + moved[1])
            before.append(jump)
            jump = cmul(jump, jump)
            k *= 2
        last = 0 if down else CHUNKS - 1
        for q in range(seqs):
            ends_ref[number, q:q + 1, 0:state] = sums[q][0][last:last + 1]
            ends_ref[number, q:q + 1, state:2 * state] = sums[q][1][last:last + 1]
        copies = []
        for k in range(1, depth):
            copy = pltpu.make_async_remote_copy(
                src_ref=ends_ref.at[number],
                dst_ref=got_ref.at[number, k - 1],
                send_sem=send_sems.at[number, k - 1],
                recv_sem=recv_sems.at[number, k - 1],
                device_id=(peer(depth - k if down else k), dp),
                device_id_type=MESH,
            )
            copy.start()
            copies.append(copy)
        place = (CHUNKS - 1 - sublane) if down else sublane
        table = (jnp.ones((CHUNKS, state), F32), zero)
        for bit, factor in enumerate(before):
            moved = cmul(table, factor)
            take = lax.rem(lax.div(place, 1 << bit), 2) == 1
            table = (jnp.where(take, moved[0], table[0]), jnp.where(take, moved[1], table[1]))
        exclusive = [(shifted(s[0], 1, down), shifted(s[1], 1, down)) for s in sums]
        return copies, jump, table, exclusive

    def finish_exchange(number, pending, down):
        copies, jump, table, exclusive = pending
        for copy in copies:
            copy.wait()
        jump_row = (jump[0][0:1], jump[1][0:1])
        carries = []
        for q in range(seqs):
            total = (jnp.zeros((1, state), F32), jnp.zeros((1, state), F32))
            factor = (jnp.ones((1, state), F32), jnp.zeros((1, state), F32))
            for k in range(1, depth):
                there = (me + k < depth) if down else (me - k >= 0)
                there = there.astype(F32)
                came = got_ref[number, k - 1]
                came = (came[q:q + 1, 0:state] * there, came[q:q + 1, state:2 * state] * there)
                moved = cmul(factor, came)
                total = (total[0] + moved[0], total[1] + moved[1])
                factor = cmul(factor, jump_row)
            wide = (jnp.broadcast_to(total[0], (CHUNKS, state)), jnp.broadcast_to(total[1], (CHUNKS, state)))
            moved = cmul(table, wide)
            carries.append((exclusive[q][0] + moved[0], exclusive[q][1] + moved[1]))
        return carries

    def wide_decay(layer):
        return tuple(jnp.broadcast_to(part[layer:layer + 1], (CHUNKS, state)) for part in decay_all)

    small_ref[...] = jnp.zeros_like(small_ref)

    for layer in range(layers):
        down = layer % 2 == 1
        decay = wide_decay(layer)
        gain = gain_ref[layer:layer + 1, :]
        skip = skip_ref[layer:layer + 1, :]
        bias = bias_ref[layer:layer + 1, :]

        def norm_tile(r, mask, carry):
            h = h_ref[layer, r, :].astype(F32)
            mean = jnp.mean(h, axis=1, keepdims=True)
            centred = h - mean
            spread_ = jnp.mean(centred * centred, axis=1, keepdims=True)
            rstd = lax.rsqrt(spread_ + EPSILON)
            xhat = centred * rstd
            xhat_ref[layer, r, :] = xhat
            rstd_ref[layer, r, :] = jnp.broadcast_to(rstd, (TILE, 128))
            normed_ref[layer, r, :] = (xhat * gain * mask).astype(BF16)
            return carry
        all_tiles(norm_tile)

        p_ref[layer] = dot(normed_ref[layer], w_ref[layer, :, 0:2 * state], NN)
        ends = scan_ends(p_ref.at[layer], decay, down)
        pending = start_exchange(layer, ends, decay, down)
        carries = finish_exchange(layer, pending, down)
        pad = pos + CHUNKS
        for q in range(seqs):
            at = q * pad + (pos if down else 0)
            z_ref[layer, at:at + CHUNKS, 0:state] = carries[q][0]
            z_ref[layer, at:at + CHUNKS, state:2 * state] = carries[q][1]

        def state_pair(i, carry):
            carry = list(carry)
            for q in range(seqs):
                pieces = []
                for half in range(2):
                    s = (steps - 1 - 2 * i - half) if down else 2 * i + half
                    r = pl.ds(pl.multiple_of(q * pos + s * CHUNKS, CHUNKS), CHUNKS)
                    add = complex_rows(p_ref.at[layer], r)
                    moved = cmul(decay, carry[q])
                    carry[q] = (moved[0] + add[0], moved[1] + add[1])
                    r = pl.ds(pl.multiple_of(q * pad + (s + (0 if down else 1)) * CHUNKS, CHUNKS), CHUNKS)
                    z_ref[layer, r, 0:state] = carry[q][0]
                    z_ref[layer, r, state:2 * state] = carry[q][1]
                    pieces.append(carry[q])
                if down:
                    pieces = pieces[::-1]
                low = (steps - 2 - 2 * i) if down else 2 * i
                r = pl.ds(pl.multiple_of(q * pos + low * CHUNKS, 2 * CHUNKS), 2 * CHUNKS)
                for part in range(2):
                    both = jnp.concatenate([pieces[0][part], pieces[1][part]], axis=0)
                    zb_ref[layer, r, part * state:(part + 1) * state] = both.astype(BF16)
            return tuple(carry)
        lax.fori_loop(0, steps // 2, state_pair, tuple(carries), unroll=2)

        tmp_ref[...] = dot(zb_ref[layer], w_ref[layer, :, 2 * state:4 * state], NT)

        def gelu_tile(r, mask, carry):
            before = tmp_ref[r, :] + skip * normed_ref[layer, r, :].astype(F32)
            phi = 0.5 * (1.0 + lax.erf(before * 0.7071067811865476))
            dg_ref[layer, r, :] = phi + before * (0.3989422804014327 * jnp.exp(-0.5 * before * before))
            gated_ref[layer, r, :] = (before * phi).astype(BF16)
            return carry
        all_tiles(gelu_tile)

        tmp_ref[...] = dot(gated_ref[layer], w_ref[layer, :, 4 * state:], NN)

        def out_tile(r, mask, carry):
            sig = 1.0 / (1.0 + jnp.exp(-(tmp_ref[r, :] + bias)))
            sig_ref[layer, r, :] = sig
            made = h_ref[layer, r, :].astype(F32) + mask * (gated_ref[layer, r, :].astype(F32) * sig)
            h_ref[layer + 1, r, :] = made.astype(BF16)
            return carry
        all_tiles(out_tile)

    gather = (lax.rem(row, steps) * CHUNKS + lax.div(row, steps) == col).astype(F32).astype(BF16)
    for q in range(seqs):
        out_ref[q] = dot(gather, h_ref[layers, seq_rows(q), :], NN).astype(BF16)

    for layer in reversed(range(layers)):
        down = layer % 2 == 1
        decay = wide_decay(layer)
        gain = gain_ref[layer:layer + 1, :]
        skip = skip_ref[layer:layer + 1, :]
        zero_row = jnp.zeros((8, model), F32)

        def gate_tile(r, mask, carry):
            sig = sig_ref[layer, r, :]
            branch = mask * go_ref[r, :].astype(F32) * sig
            grad = (branch * gated_ref[layer, r, :].astype(F32) * (1.0 - sig)).astype(BF16)
            gg_ref[r, :] = grad
            acc_ref[r, :] = branch
            return carry + fold(grad.astype(F32))
        bias_sum = all_tiles(gate_tile, zero_row)
        tmp_ref[...] = dot(gg_ref[...], w_ref[layer, :, 4 * state:], NT)

        def before_tile(r, mask, carry):
            gated_grad = (acc_ref[r, :] + tmp_ref[r, :]).astype(BF16).astype(F32)
            grad = (gated_grad * dg_ref[layer, r, :]).astype(BF16)
            gb_ref[r, :] = grad
            return carry + fold(grad.astype(F32) * normed_ref[layer, r, :].astype(F32))
        skip_sum = all_tiles(before_tile, zero_row)

        src_ref[...] = dot(gb_ref[...], w_ref[layer, :, 2 * state:4 * state], NN)
        back = conj(decay)
        ends = scan_ends(src_ref, back, not down)
        pending = start_exchange(layers + layer, ends, back, not down)
        gpart_ref[layer, :, 4 * state:] = dot(gated_ref[layer], gg_ref[...], TN)
        gpart_ref[layer, :, 2 * state:4 * state] = dot(gb_ref[...], zb_ref[layer], TN)
        carries = finish_exchange(layers + layer, pending, not down)

        def adjoint_pair(i, loop):
            carry, sums = list(loop[0]), list(loop[1])
            for q in range(seqs):
                pieces = []
                for half in range(2):
                    s = 2 * i + half if down else (steps - 1 - 2 * i - half)
                    r = pl.ds(pl.multiple_of(q * pos + s * CHUNKS, CHUNKS), CHUNKS)
                    add = complex_rows(src_ref, r)
                    moved = cmul(back, carry[q])
                    adj = (moved[0] + add[0], moved[1] + add[1])
                    carry[q] = adj
                    pieces.append(adj)
                    proj = complex_rows(p_ref.at[layer], r)
                    r = pl.ds(pl.multiple_of(q * pad + (s + (1 if down else 0)) * CHUNKS, CHUNKS), CHUNKS)
                    prior = complex_rows(z_ref.at[layer], r)
                    sums[0] = sums[0] + (adj[0] * prior[0] + adj[1] * prior[1])
                    sums[1] = sums[1] + (adj[1] * prior[0] - adj[0] * prior[1])
                    sums[2] = sums[2] + (adj[0] * proj[0] + adj[1] * proj[1])
                    sums[3] = sums[3] + (adj[1] * proj[0] - adj[0] * proj[1])
                if not down:
                    pieces = pieces[::-1]
                low = 2 * i if down else (steps - 2 - 2 * i)
                r = pl.ds(pl.multiple_of(q * pos + low * CHUNKS, 2 * CHUNKS), 2 * CHUNKS)
                for part in range(2):
                    both = jnp.concatenate([pieces[0][part], pieces[1][part]], axis=0)
                    gp_ref[r, part * state:(part + 1) * state] = both.astype(BF16)
            return tuple(carry), tuple(sums)
        _, sums = lax.fori_loop(0, steps // 2, adjoint_pair, (tuple(carries), (zero,) * 4), unroll=1)

        gpart_ref[layer, :, 0:2 * state] = dot(normed_ref[layer], gp_ref[...], TN)
        tmp_ref[...] = dot(gp_ref[...], w_ref[layer, :, 0:2 * state], NT)

        def input_tile(r, mask, carry):
            grad = (tmp_ref[r, :] + skip * gb_ref[r, :].astype(F32)) * mask
            xhat = xhat_ref[layer, r, :]
            rstd = jnp.concatenate([rstd_ref[layer, r, :]] * (model // 128), axis=1)
            scaled = grad * gain
            first = jnp.mean(scaled, axis=1, keepdims=True)
            second = jnp.mean(scaled * xhat, axis=1, keepdims=True)
            made = go_ref[r, :].astype(F32) + rstd * (scaled - first - xhat * second)
            go_ref[r, :] = made.astype(BF16)
            return carry + fold(grad * xhat)
        gain_sum = all_tiles(input_tile, zero_row)

        for at, value in enumerate((gain_sum, skip_sum, bias_sum)):
            small_ref[layer, at:at + 1, :] = jnp.sum(value, axis=0, keepdims=True)
        for at, value in enumerate(sums):
            small_ref[layer, 3 + at:4 + at, 0:state] = jnp.sum(value, axis=0, keepdims=True)

    for q in range(seqs):
        xg_ref[q] = dot(gather, go_ref[seq_rows(q), :], NN).astype(BF16)


def run_main(depth, x_in, lengths, cotangent, norm_gain, lambda_re, lambda_im, log_step, weights, skip_weight, glu_bias):
    seqs, pos, model = x_in.shape
    layers, state = lambda_re.shape
    rows = seqs * pos
    wide = weights.shape[2]
    vmem = pl.BlockSpec(memory_space=pltpu.VMEM)
    smem = pl.BlockSpec(memory_space=pltpu.SMEM)
    return pl.pallas_call(
        functools.partial(main_kernel, depth),
        out_shape=(
            jax.ShapeDtypeStruct(x_in.shape, BF16),
            jax.ShapeDtypeStruct(x_in.shape, BF16),
            jax.ShapeDtypeStruct((layers, model, wide), F32),
            jax.ShapeDtypeStruct((layers, 8, model), F32),
        ),
        in_specs=[vmem, vmem, smem] + [vmem] * 7,
        out_specs=(vmem,) * 4,
        scratch_shapes=[
            pltpu.VMEM((layers + 1, rows, model), BF16),
            pltpu.VMEM((rows, model), BF16),
            pltpu.VMEM((layers, rows, model), F32),
            pltpu.VMEM((layers, rows, 128), F32),
            pltpu.VMEM((layers, rows, model), BF16),
            pltpu.VMEM((layers, rows, 2 * state), F32),
            pltpu.VMEM((layers, rows + seqs * CHUNKS, 2 * state), F32),
            pltpu.VMEM((layers, rows, 2 * state), BF16),
            pltpu.VMEM((layers, rows, model), F32),
            pltpu.VMEM((layers, rows, model), BF16),
            pltpu.VMEM((layers, rows, model), F32),
            pltpu.VMEM((rows, model), BF16),
            pltpu.VMEM((rows, model), BF16),
            pltpu.VMEM((rows, 2 * state), BF16),
            pltpu.VMEM((rows, 2 * state), F32),
            pltpu.VMEM((rows, model), F32),
            pltpu.VMEM((rows, model), F32),
            pltpu.VMEM((2 * layers, 8, 2 * state), F32),
            pltpu.VMEM((2 * layers, depth - 1, 8, 2 * state), F32),
            pltpu.SemaphoreType.DMA((2 * layers, depth - 1)),
            pltpu.SemaphoreType.DMA((2 * layers, depth - 1)),
        ],
        compiler_params=pltpu.CompilerParams(
            collective_id=0, has_side_effects=True, vmem_limit_bytes=60 * 2**20
        ),
    )(x_in, cotangent, lengths, norm_gain, lambda_re, lambda_im, log_step, skip_weight, glu_bias, weights)


def per_device(
    x_in, lengths, cotangent, norm_gain, lambda_re, lambda_im, log_step,
    b_weight, c_weight, skip_weight, glu_weight, glu_bias,
):
    depth = lax.axis_size("pipe")
    state = lambda_re.shape[1]
    _, _, coef = discretize(lambda_re, lambda_im, log_step)
    c_real, c_imag = c_weight[:, :, :state], c_weight[:, :, state:]
    turned = cmul((coef[0][:, None], coef[1][:, None]), (c_real, c_imag))
    shard = jnp.concatenate([b_weight, turned[0], -turned[1], glu_weight], axis=2).astype(BF16)
    weights = lax.all_gather(shard, "dp", axis=1, tiled=True)
    output, x_grad, gpart, small = run_main(
        depth, x_in, lengths, cotangent, norm_gain, lambda_re, lambda_im, log_step, weights, skip_weight, glu_bias
    )
    grads = lax.psum_scatter(gpart, "dp", scatter_dimension=1, tiled=True)
    grads = lax.psum(grads.astype(BF16), "pipe").astype(F32)
    small = lax.psum(small, ("pipe", "dp"))
    m_real, m_imag = grads[:, :, 2 * state:3 * state], grads[:, :, 3 * state:4 * state]
    turned = cmul((coef[0][:, None], coef[1][:, None]), (m_real, m_imag))
    c_grad = jnp.concatenate([turned[0], -turned[1]], axis=2)
    decay_grad = (small[:, 3, :state], small[:, 4, :state])
    scale = coef[0] * coef[0] + coef[1] * coef[1]
    coef_grad = cmul((small[:, 5, :state], small[:, 6, :state]), (coef[0] / scale, coef[1] / scale))
    lam_re_grad, lam_im_grad, step_grad = discretize_grads(lambda_re, lambda_im, log_step, decay_grad, coef_grad)
    return (
        output, x_grad, small[:, 0], lam_re_grad, lam_im_grad, step_grad,
        grads[:, :, :2 * state], c_grad, small[:, 1], grads[:, :, 4 * state:], small[:, 2],
    )


def solution(mesh):
    split, whole, rows = P("dp", "pipe", None), P(), P(None, "dp", None)
    return jax.shard_map(
        per_device,
        mesh=mesh,
        in_specs=(split, P("dp"), split, whole, whole, whole, whole, rows, rows, whole, rows, whole),
        out_specs=(split, split, whole, whole, whole, whole, rows, rows, whole, rows, whole),
        check_vma=False,
    )
```

time: 2970 us -> 259 us (0.09); the launches traced: 2910 us -> 259 us
  local copies, waits for them, and re-layouts: 1170 us -> 6.81 us
  waiting for transfers between devices: 937 us -> 140 us
  other arithmetic: 364 us -> 10.1 us
  starting transfers between devices: 248 us -> 0.12 us
  matrix products: 53.5 us -> 0 us
  Pallas kernels: 0 us -> 48.5 us
  blocking collectives: 87.8 us -> 39.6 us
  loops' own time: 41.1 us -> 0 us
    ppermute x16 -> x0, waiting for transfers between devices: 875 us -> none  [shifted(): lax.ppermute(value, axis, [(source, source + steps) for source in range(f...]
    rev x32 -> x0, local copies, waits for them, and re-layouts: 401 us -> none  [the longest x24 298 us: in_order(): return jnp.where(reverse_flag, jnp.flip(values, 0), values)]
    slice x250 -> x4, local copies, waits for them, and re-layouts: 251 us -> 3.35 us  [the longest x1 1.7 us: per_device(): grads[:, :, :2 * state]]
    ppermute x16 -> x0, starting transfers between devices: 239 us -> none  [shifted(): lax.ppermute(value, axis, [(source, source + steps) for source in range(f...]
    another operation x243 -> x0, local copies, waits for them, and re-layouts: 171 us -> none  [the longest x96 50.7 us: chained_scan(): table_imag = jnp.stack(powers_imag, axis=0)]
    add x195 -> x0, other arithmetic: 164 us -> none  [the longest x70 68.9 us: chained_scan(): lax.associative_scan(compose, (jump_real, jump_imag, ends_real, ends_imag))]
    pad x96 -> x0, local copies, waits for them, and re-layouts: 116 us -> none  [chained_scan(): lax.associative_scan(compose, (jump_real, jump_imag, ends_real, ends_imag))]
    add x86 -> x0, local copies, waits for them, and re-layouts: 101 us -> none  [the longest x56 67 us: chained_scan(): decay_real * run_real - decay_imag * run_imag + block_real[:, offset]]
  transfers between devices with their start and end apart: 24 -> 3, of which waited for: 19 -> 3; matrix products, arithmetic and copies ran while one was open for 9% -> 1% of each run, Pallas kernels for 0% -> 0%
where the time goes in v1:
time: 259 us
  waiting for transfers between devices  140 us (54%)
  Pallas kernels  48.5 us (19%)
  blocking collectives  39.6 us (15%)
  between operations  13.8 us (5%)
  other arithmetic  10.1 us (4%)
  local copies, waits for them, and re-layouts  6.81 us (3%)
    all_gather x1, waiting for transfers between devices, per_device(): weights = lax.all_gather(shard, 'dp', axis=1, tiled=True)  50 us
    pallas_call x1, Pallas kernels, run_main(): pl.pallas_call(functools.partial(main_kernel, depth), out_shape=(jax.Shap...  48.5 us
    reduce_scatter x1, waiting for transfers between devices, per_device(): grads = lax.psum_scatter(gpart, 'dp', scatter_dimension=1, tiled=True)  47.4 us
    psum x1, waiting for transfers between devices, per_device(): grads = lax.psum(grads.astype(BF16), 'pipe').astype(F32)  42.7 us
    psum x1, blocking collectives, per_device(): small = lax.psum(small, ('pipe', 'dp'))  39.6 us
  transfers between devices with their start and end apart: 3, of which 3 were waited for; matrix products, arithmetic and copies ran while one was open for 1% of the time, Pallas kernels for 0%

profile of v1, /device:TPU:0, one launch (start us, length us, event | category | flops | bytes accessed | tf_op | source)
XLA Modules:
  0.0 259.0 jit_solution(15805627538684392572)
XLA Ops:
  7.2 1.0 convert.15
  8.2 1.0 convert.12
  9.2 0.8 fusion.3
  10.0 1.1 subtract_convert_fusion
  11.1 0.9 pad_maximum_fusion
  12.0 0.0 reduce-scatter.2.cloned.1.call-start
  12.0 50.0 %all-gather.2.cloned.1.call-done.w_ref = bf16[2,512,2048]{2,1,0:T(8,128)(2,1)} async-done(((bf16[2,64,2048]{2,1,0:T(8,128)(2,1)}), bf16[2,512,2048]{2,1,0:T(8,128)(2,1)}) %all-gather.2.cloned.1.call-update) | async-done | bytes 4194320 | tf_op jit(solution)/shard_map/all_gather | solution.py:423
  62.0 48.5 %shard_map.203 = (bf16[2,256,512]{2,1,0:T(8,128)(2,1)}, bf16[2,256,512]{2,1,0:T(8,128)(2,1)}, f32[2,512,2048]{2,1,0:T(8,128)}, f32[2,8,512]{2,1,0:T(8,128)}) custom-call(bf16[2,256,512]{2,1,0:T(8,128)(2,1)} %x_ref.1, bf16[2,256,512]{2,1,0:T(8,128)(2,1)} %cot_ref.1, s32[2]{0:T(128)} %len_ref.1, f32[2,512]{1,0:T(2,128)} %gain_ref.1, f32[2,384]{1,0:T(2,128)} %lre_ref.1, ...), custom_call_target="tpu_custom_call" | custom-call | tf_op jit(solution)/shard_map/pallas_call | solution.py:374
  110.6 0.7 copy-done.5
  111.2 39.6 %psum.14 = f32[2,8,512]{2,1,0:T(8,128)S(1)} all-reduce(f32[2,8,512]{2,1,0:T(8,128)S(1)} %copy-done.5), channel_id=1, replica_groups=mesh['pipe'=4,'dp'=8] {'pipe','dp'}, use_global_device_ids=true, to_apply=%region_0.0 | all-reduce | flops 8192 | bytes 65536 | tf_op jit(solution)/shard_map/psum | solution.py:429
  150.9 47.4 %reduce-scatter.2.cloned.1.call-done = f32[2,64,2048]{2,1,0:T(8,128)} async-done(((f32[2,512,2048]{2,1,0:T(8,128)}), f32[2,64,2048]{2,1,0:T(8,128)}) %reduce-scatter.2.cloned.1.call-update) | async-done | bytes 1048592 | tf_op jit(solution)/shard_map/reduce_scatter | solution.py:427
  198.3 2.1 convert_element_type.7
  200.4 0.6 copy_bitcast_fusion
  201.0 0.6 copy.56
  201.6 0.7 subtract_multiply_fusion
  202.3 0.7 add_subtract_fusion
  202.9 42.7 %all-reduce.2.cloned.1.call-done = bf16[2,64,2048]{2,1,0:T(8,128)(2,1)} async-done(((bf16[2,64,2048]{2,1,0:T(8,128)(2,1)}), bf16[2,64,2048]{2,1,0:T(8,128)(2,1)}) %all-reduce.2.cloned.1.call-update) | async-done | bytes 524304 | tf_op jit(solution)/shard_map/psum | solution.py:428
  245.6 1.1 convert_element_type.8
  246.7 0.1 multiply_subtract_fusion
  246.8 0.8 pad_maximum_fusion.1
  247.6 1.6 slice.61
  249.2 1.7 slice.57
  250.9 0.8 copy.60
  251.7 0.8 copy.61
  (18 shorter events, 0.2 us)
Async XLA Ops:
  7.2 54.8 %all-gather.2.cloned.1.call-start = ((), (), s32[]{:S(2)}) async-start(), calls=%async_computation.1 | async-start | bytes 4718592 | tf_op jit(solution)/shard_map/all_gather | solution.py:423
  12.0 189.6 %copy-start.2 = (f32[2,384]{1,0:T(2,128)S(1)}, f32[2,384]{1,0:T(2,128)}, u32[]{:S(2)}) copy-start(f32[2,384]{1,0:T(2,128)} %lre_ref.1) | copy-start | bytes 9220
  12.0 189.6 %copy-start.3 = (f32[2,384]{1,0:T(2,128)S(1)}, f32[2,384]{1,0:T(2,128)}, u32[]{:S(2)}) copy-start(f32[2,384]{1,0:T(2,128)} %lim_ref.1) | copy-start | bytes 9220
  12.0 189.6 %copy-start.4 = (f32[2,384]{1,0:T(2,128)S(1)}, f32[2,384]{1,0:T(2,128)}, u32[]{:S(2)}) copy-start(f32[2,384]{1,0:T(2,128)} %lst_ref.1) | copy-start | bytes 9220
  12.0 186.3 %reduce-scatter.2.cloned.1.call-start = ((), (), s32[]{:S(2)}) async-start(), calls=%async_computation.2 | async-start | bytes 9437184 | tf_op jit(solution)/shard_map/reduce_scatter | solution.py:427
  110.5 0.8 copy-start.5
  110.5 140.4 %copy-start.1 = (bf16[2,256,512]{2,1,0:T(8,128)(2,1)S(1)}, bf16[2,256,512]{2,1,0:T(8,128)(2,1)}, u32[]{:S(2)}) copy-start(bf16[2,256,512]{2,1,0:T(8,128)(2,1)} %get-tuple-element.54) | copy-start | bytes 1572868
  110.5 141.2 %copy-start = (bf16[2,256,512]{2,1,0:T(8,128)(2,1)S(1)}, bf16[2,256,512]{2,1,0:T(8,128)(2,1)}, u32[]{:S(2)}) copy-start(bf16[2,256,512]{2,1,0:T(8,128)(2,1)} %get-tuple-element.55) | copy-start | bytes 1572868
  110.5 135.0 %all-reduce.2.cloned.1.call-start = ((), (), s32[]{:S(2)}) async-start(), calls=%async_computation.3 | async-start | bytes 1048576 | tf_op jit(solution)/shard_map/psum | solution.py:428
Sparse Core Ops, SparseCore 0:
  12.1 49.8 all-gather.1
  110.7 87.5 reduce-scatter.1
  201.9 43.6 all-reduce.1

commit v2 on v1

--- a/solution.py
+++ b/solution.py
@@ -56,27 +56,196 @@
     return first[0] - second[0], first[1] - second[1], step * turned[0]
 
 
-def main_kernel(
-    depth,
-    x_ref, cot_ref, len_ref, gain_ref, lre_ref, lim_ref, lst_ref, skip_ref, bias_ref, w_ref,
-    out_ref, xg_ref, gpart_ref, small_ref,
-    h_ref, go_ref, xhat_ref, rstd_ref, normed_ref, p_ref, z_ref, zb_ref, dg_ref, gated_ref, sig_ref,
-    gg_ref, gb_ref, gp_ref, src_ref, tmp_ref, acc_ref,
-    ends_ref, got_ref, send_sems, recv_sems,
-):
+def weight_gather(refs, pieces, depth, planes, me, plane, core, at_pipe, at_plane, at_core, remote):
+    w_ref = refs["w"]
+    sems = (refs["w_send"], refs["w_recv"])
+    along, onward, across = {}, {}, {}
+
+    def part(piece):
+        layer, low, high = pieces[piece]
+        return w_ref.at[layer], pl.ds(low, high - low)
+
+    def send(piece):
+        ref, cols = part(piece)
+        along[piece] = []
+        for k in range(1, planes):
+            block = ref.at[plane, core, me, :, cols]
+            along[piece].append(remote(block, block, sems, (piece, k - 1), at_plane(k)))
+
+    def relay(piece):
+        ref, cols = part(piece)
+        onward[piece] = []
+        for k in range(1, planes):
+            along[piece][k - 1].wait_recv()
+            block = ref.at[lax.rem(plane - k + planes, planes), core, me, :, cols]
+            for j in range(1, depth):
+                at = planes - 1 + (k - 1) * (depth - 1) + j - 1
+                onward[piece].append(remote(block, block, sems, (piece, at), at_pipe(j)))
+
+    def swap(piece):
+        ref, cols = part(piece)
+        for copy in onward[piece]:
+            copy.wait_recv()
+        block = ref.at[:, core, :, :, cols]
+        across[piece] = remote(block, block, sems, (piece, planes * depth - 1), at_core)
+
+    def ready(piece):
+        across[piece].wait_recv()
+
+    return send, relay, swap, ready
+
+
+def gradient_sums(refs, kinds, depth, planes, me, plane, core, at_pipe, at_plane, at_core, remote):
+    sems = (refs["g_send"], refs["g_recv"])
+    copies = {}
+
+    def of(name, piece):
+        return refs[name + str(piece % kinds)].at[piece // kinds]
+
+    def stage(piece, matrix, low, high):
+        part = of("part", piece)
+        part[..., low:high] = matrix.astype(BF16).reshape(part.shape[:-1] + (high - low,))
+
+    def start(piece):
+        part, other = of("part", piece), of("other", piece)
+        copies[piece, 0] = remote(part.at[:, 1 - core], other, sems, (piece, 0), at_core)
+
+    def to_pipe(piece):
+        copies[piece, 0].wait_recv()
+        part, other, pair = of("part", piece), of("other", piece), of("pair", piece)
+
+        def add(i, carry):
+            z, j = lax.div(i, depth), lax.rem(i, depth)
+            pair[j, z] = (part[z, core, j].astype(F32) + other[z, j].astype(F32)).astype(BF16)
+            return carry
+        lax.fori_loop(0, planes * depth, add, 0)
+        copies[piece, 1] = [
+            remote(pair.at[lax.rem(me + k, depth)], of("quad", piece).at[k - 1], sems, (piece, k), at_pipe(k))
+            for k in range(1, depth)
+        ]
+
+    def to_plane(piece):
+        pair, quad, line = of("pair", piece), of("quad", piece), of("line", piece)
+        for copy in copies[piece, 1]:
+            copy.wait_recv()
+
+        def add(z, carry):
+            total = pair[me, z].astype(F32)
+            for k in range(1, depth):
+                total = total + quad[k - 1, z].astype(F32)
+            line[z] = total.astype(BF16)
+            return carry
+        lax.fori_loop(0, planes, add, 0)
+        copies[piece, 2] = [
+            remote(line.at[lax.rem(plane + k, planes)], of("came", piece).at[k - 1], sems, (piece, depth + k - 1), at_plane(k))
+            for k in range(1, planes)
+        ]
+
+    def to_peers(piece):
+        line, came, done = of("line", piece), of("came", piece), of("done", piece)
+        for copy in copies[piece, 2]:
+            copy.wait_recv()
+        total = line[plane].astype(F32)
+        for k in range(1, planes):
+            total = total + came[k - 1].astype(F32)
+        done[me] = total.astype(BF16)
+        copies[piece, 3] = [
+            remote(done.at[me], done.at[me], sems, (piece, depth + planes + k - 2), at_pipe(k))
+            for k in range(1, depth)
+        ]
+
+    def finish(piece):
+        for copy in copies[piece, 3]:
+            copy.wait_recv()
+        done = of("done", piece)[...]
+        return done.reshape(done.shape[0] * done.shape[1], done.shape[2])
+
+    return stage, start, to_pipe, to_plane, to_peers, finish
+
+
+def small_sums(refs, depth, planes, me, plane, core, at_pipe, at_plane, at_core, remote):
+    sems = (refs["s_send"], refs["s_recv"])
+    own, other, quad, line = refs["small"], refs["s_other"], refs["s_quad"], refs["s_line"]
+    copies = {}
+
+    def start(layer):
+        copies[layer, 0] = remote(own.at[layer], other.at[layer], sems, (layer, 0), at_core)
+
+    def to_pipe(layer):
+        copies[layer, 0].wait_recv()
+        quad[layer, me] = own[layer] + other[layer]
+        copies[layer, 1] = [
+            remote(quad.at[layer, me], quad.at[layer, me], sems, (layer, k), at_pipe(k)) for k in range(1, depth)
+        ]
+
+    def to_plane(layer):
+        for copy in copies[layer, 1]:
+            copy.wait_recv()
+        total = quad[layer, 0]
+        for j in range(1, depth):
+            total = total + quad[layer, j]
+        line[layer, plane] = total
+        copies[layer, 2] = [
+            remote(line.at[layer, plane], line.at[layer, plane], sems, (layer, depth + k - 1), at_plane(k))
+            for k in range(1, planes)
+        ]
+
+    def finish(layer):
+        for copy in copies[layer, 2]:
+            copy.wait_recv()
+        total = line[layer, 0]
+        for z in range(1, planes):
+            total = total + line[layer, z]
+        return total
+
+    return start, to_pipe, to_plane, finish
+
+
+def main_kernel(depth, planes, names, *refs):
+    r_ = dict(zip(names, refs))
+    x_ref, cot_ref, len_ref, gain_ref = r_["x"], r_["cot"], r_["len"], r_["gain"]
+    lre_ref, lim_ref, lst_ref, skip_ref, bias_ref = r_["lre"], r_["lim"], r_["lst"], r_["skip"], r_["bias"]
+    out_ref, xg_ref, small_ref = r_["out"], r_["xg"], r_["small"]
+    h_ref, go_ref, xhat_ref, rstd_ref, normed_ref = r_["h"], r_["go"], r_["xhat"], r_["rstd"], r_["normed"]
+    p_ref, z_ref, zb_ref, dg_ref, gated_ref, sig_ref = r_["p"], r_["z"], r_["zb"], r_["dg"], r_["gated"], r_["sig"]
+    gg_ref, gb_ref, gp_ref, src_ref, tmp_ref, acc_ref = r_["gg"], r_["gb"], r_["gp"], r_["src"], r_["tmp"], r_["acc"]
+    ends_ref, got_ref, send_sems, recv_sems = r_["ends"], r_["got"], r_["send"], r_["recv"]
+    w_ref = r_["w"]
     seqs, pos, model = x_ref.shape
     state = lre_ref.shape[1]
     layers = gain_ref.shape[0]
     rows = seqs * pos
     steps = pos // CHUNKS
     me, dp = lax.axis_index("pipe"), lax.axis_index("dp")
+    plane, core = lax.div(dp, 2), lax.rem(dp, 2)
 
     def peer(k):
         return lax.rem(me + k, depth)
 
+    def at_pipe(k):
+        return (peer(k), dp)
+
+    def at_plane(k):
+        return (me, 2 * lax.rem(plane + k, planes) + core)
+
+    at_core = (me, 2 * plane + (1 - core))
+    others = [at_pipe(k) for k in range(1, depth)]
+    if planes:
+        others += [at_plane(k) for k in range(1, planes)] + [at_core]
     barrier = pltpu.get_barrier_semaphore()
-    for k in range(1, depth):
-        pl.semaphore_signal(barrier, inc=1, device_id=(peer(k), dp), device_id_type=MESH)
+    for device in others:
+        pl.semaphore_signal(barrier, inc=1, device_id=device, device_id_type=MESH)
+
+    unsent = []
+
+    def remote(src, dst, sems, at, device):
+        copy = pltpu.make_async_remote_copy(
+            src_ref=src, dst_ref=dst, send_sem=sems[0].at[at], recv_sem=sems[1].at[at],
+            device_id=device, device_id_type=MESH,
+        )
+        copy.start()
+        unsent.append(copy)
+        return copy
 
     row = lax.broadcasted_iota(jnp.int32, (pos, pos), 0)
     col = lax.broadcasted_iota(jnp.int32, (pos, pos), 1)
@@ -103,12 +272,35 @@
             total = total + value[r:r + 8]
         return total
 
+    step_all, decay_all, coef_all = discretize(lre_ref[...], lim_ref[...], lst_ref[...])
+    if planes:
+        ways = (depth, planes, me, plane, core, at_pipe, at_plane, at_core, remote)
+        pieces = ((0, 0, 2 * state), (0, 2 * state, 4 * state + model), (1, 0, 4 * state + model))
+        w_send, w_relay, w_swap, w_ready = weight_gather(r_, pieces, *ways)
+        g_stage, g_start, g_pipe, g_plane, g_peers, g_finish = gradient_sums(r_, 2, *ways)
+        s_start, s_pipe, s_plane, s_finish = small_sums(r_, *ways)
+        for layer in range(layers):
+            own = w_ref.at[layer, plane, core]
+
+            def keep(matrix, low):
+                high = low + matrix.shape[1]
+                own[:, :, low:high] = matrix.astype(BF16).reshape(depth, matrix.shape[0] // depth, high - low)
+            keep(r_["b"][layer], 0)
+            coef = (coef_all[0][layer:layer + 1], coef_all[1][layer:layer + 1])
+            turned = cmul(coef, (r_["c"][layer, :, 0:state], r_["c"][layer, :, state:2 * state]))
+            keep(turned[0], 2 * state)
+            keep(-turned[1], 3 * state)
+            keep(r_["glu"][layer], 4 * state)
+    pl.semaphore_wait(barrier, len(others))
+    if planes:
+        w_send(0)
     for q in range(seqs):
         h_ref[0, seq_rows(q), :] = dot(spread, x_ref[q], NN).astype(BF16)
-        go_ref[seq_rows(q), :] = dot(spread, cot_ref[q], NN).astype(BF16)
-
-    step_all, decay_all, coef_all = discretize(lre_ref[...], lim_ref[...], lst_ref[...])
-    pl.semaphore_wait(barrier, depth - 1)
+
+    def matrix(layer, which):
+        low, high = (0, 2 * state, 4 * state)[which], (2 * state, 4 * state, w_ref.shape[-1])[which]
+        value = w_ref[layer, ..., low:high]
+        return value.reshape(model, high - low)
 
     def complex_rows(src, r):
         return (src[r, 0:state], src[r, state:2 * state])
@@ -153,18 +345,11 @@
         for q in range(seqs):
             ends_ref[number, q:q + 1, 0:state] = sums[q][0][last:last + 1]
             ends_ref[number, q:q + 1, state:2 * state] = sums[q][1][last:last + 1]
-        copies = []
-        for k in range(1, depth):
-            copy = pltpu.make_async_remote_copy(
-                src_ref=ends_ref.at[number],
-                dst_ref=got_ref.at[number, k - 1],
-                send_sem=send_sems.at[number, k - 1],
-                recv_sem=recv_sems.at[number, k - 1],
-                device_id=(peer(depth - k if down else k), dp),
-                device_id_type=MESH,
-            )
-            copy.start()
-            copies.append(copy)
+        copies = [
+            remote(ends_ref.at[number], got_ref.at[number, k - 1], (send_sems, recv_sems), (number, k - 1),
+                   at_pipe(depth - k if down else k))
+            for k in range(1, depth)
+        ]
         place = (CHUNKS - 1 - sublane) if down else sublane
         table = (jnp.ones((CHUNKS, state), F32), zero)
         for bit, factor in enumerate(before):
@@ -177,7 +362,7 @@
     def finish_exchange(number, pending, down):
         copies, jump, table, exclusive = pending
         for copy in copies:
-            copy.wait()
+            copy.wait_recv()
         jump_row = (jump[0][0:1], jump[1][0:1])
         carries = []
         for q in range(seqs):
@@ -221,9 +406,26 @@
             return carry
         all_tiles(norm_tile)
 
-        p_ref[layer] = dot(normed_ref[layer], w_ref[layer, :, 0:2 * state], NN)
+        if planes and layer == 0:
+            w_relay(0)
+            w_send(1)
+        if layer == 0:
+            for q in range(seqs):
+                go_ref[seq_rows(q), :] = dot(spread, cot_ref[q], NN).astype(BF16)
+        if planes and layer == 0:
+            w_swap(0)
+            w_relay(1)
+            w_send(2)
+            w_ready(0)
+        if planes and layer == 1:
+            w_swap(2)
+            w_ready(2)
+
+        p_ref[layer] = dot(normed_ref[layer], matrix(layer, 0), NN)
         ends = scan_ends(p_ref.at[layer], decay, down)
         pending = start_exchange(layer, ends, decay, down)
+        if planes and layer == 0:
+            w_relay(2)
         carries = finish_exchange(layer, pending, down)
         pad = pos + CHUNKS
         for q in range(seqs):
@@ -255,7 +457,10 @@
             return tuple(carry)
         lax.fori_loop(0, steps // 2, state_pair, tuple(carries), unroll=2)
 
-        tmp_ref[...] = dot(zb_ref[layer], w_ref[layer, :, 2 * state:4 * state], NT)
+        if planes and layer == 0:
+            w_swap(1)
+            w_ready(1)
+        tmp_ref[...] = dot(zb_ref[layer], matrix(layer, 1), NT)
 
         def gelu_tile(r, mask, carry):
             before = tmp_ref[r, :] + skip * normed_ref[layer, r, :].astype(F32)
@@ -265,7 +470,7 @@
             return carry
         all_tiles(gelu_tile)
 
-        tmp_ref[...] = dot(gated_ref[layer], w_ref[layer, :, 4 * state:], NN)
+        tmp_ref[...] = dot(gated_ref[layer], matrix(layer, 2), NN)
 
         def out_tile(r, mask, carry):
             sig = 1.0 / (1.0 + jnp.exp(-(tmp_ref[r, :] + bias)))
@@ -294,7 +499,7 @@
             acc_ref[r, :] = branch
             return carry + fold(grad.astype(F32))
         bias_sum = all_tiles(gate_tile, zero_row)
-        tmp_ref[...] = dot(gg_ref[...], w_ref[layer, :, 4 * state:], NT)
+        tmp_ref[...] = dot(gg_ref[...], matrix(layer, 2), NT)
 
         def before_tile(r, mask, carry):
             gated_grad = (acc_ref[r, :] + tmp_ref[r, :]).astype(BF16).astype(F32)
@@ -303,12 +508,21 @@
             return carry + fold(grad.astype(F32) * normed_ref[layer, r, :].astype(F32))
         skip_sum = all_tiles(before_tile, zero_row)
 
-        src_ref[...] = dot(gb_ref[...], w_ref[layer, :, 2 * state:4 * state], NN)
+        src_ref[...] = dot(gb_ref[...], matrix(layer, 1), NN)
         back = conj(decay)
         ends = scan_ends(src_ref, back, not down)
         pending = start_exchange(layers + layer, ends, back, not down)
-        gpart_ref[layer, :, 4 * state:] = dot(gated_ref[layer], gg_ref[...], TN)
-        gpart_ref[layer, :, 2 * state:4 * state] = dot(gb_ref[...], zb_ref[layer], TN)
+        glu_part = dot(gated_ref[layer], gg_ref[...], TN)
+        c_part = dot(gb_ref[...], zb_ref[layer], TN)
+        if planes:
+            g_stage(2 * layer, c_part, 0, 2 * state)
+            g_stage(2 * layer, glu_part, 2 * state, 2 * state + model)
+            g_start(2 * layer)
+            if layer == 0:
+                g_plane(2)
+        else:
+            r_["gpart"][layer, :, 4 * state:] = glu_part
+            r_["gpart"][layer, :, 2 * state:4 * state] = c_part
         carries = finish_exchange(layers + layer, pending, not down)
 
         def adjoint_pair(i, loop):
@@ -340,8 +554,17 @@
             return tuple(carry), tuple(sums)
         _, sums = lax.fori_loop(0, steps // 2, adjoint_pair, (tuple(carries), (zero,) * 4), unroll=1)
 
-        gpart_ref[layer, :, 0:2 * state] = dot(normed_ref[layer], gp_ref[...], TN)
-        tmp_ref[...] = dot(gp_ref[...], w_ref[layer, :, 0:2 * state], NT)
+        b_part = dot(normed_ref[layer], gp_ref[...], TN)
+        if planes:
+            g_stage(2 * layer + 1, b_part, 0, 2 * state)
+            g_start(2 * layer + 1)
+            g_pipe(2 * layer)
+            if layer == 0:
+                g_plane(3)
+                g_peers(2)
+        else:
+            r_["gpart"][layer, :, 0:2 * state] = b_part
+        tmp_ref[...] = dot(gp_ref[...], matrix(layer, 0), NT)
 
         def input_tile(r, mask, carry):
             grad = (tmp_ref[r, :] + skip * gb_ref[r, :].astype(F32)) * mask
@@ -359,70 +582,153 @@
             small_ref[layer, at:at + 1, :] = jnp.sum(value, axis=0, keepdims=True)
         for at, value in enumerate(sums):
             small_ref[layer, 3 + at:4 + at, 0:state] = jnp.sum(value, axis=0, keepdims=True)
+        if planes:
+            s_start(layer)
+            g_pipe(2 * layer + 1)
+            s_pipe(layer)
 
     for q in range(seqs):
         xg_ref[q] = dot(gather, go_ref[seq_rows(q), :], NN).astype(BF16)
-
-
-def run_main(depth, x_in, lengths, cotangent, norm_gain, lambda_re, lambda_im, log_step, weights, skip_weight, glu_bias):
+    if not planes:
+        for copy in unsent:
+            copy.wait_send()
+        return
+    g_peers(3)
+    g_plane(0)
+    s_plane(1)
+    g_plane(1)
+    s_plane(0)
+    g_peers(0)
+    g_peers(1)
+
+    def store_small(layer):
+        total = s_finish(layer)
+        for at, name in enumerate(("gain_grad", "skip_grad", "bias_grad")):
+            r_[name][layer:layer + 1, :] = total[at:at + 1, :]
+        one = slice(layer, layer + 1)
+        coef = (coef_all[0][one], coef_all[1][one])
+        sums = [total[at:at + 1, 0:state] for at in range(3, 7)]
+        scale = coef[0] * coef[0] + coef[1] * coef[1]
+        coef_grad = cmul((sums[2], sums[3]), (coef[0] / scale, coef[1] / scale))
+        made = discretize_grads(lre_ref[one], lim_ref[one], lst_ref[one], (sums[0], sums[1]), coef_grad)
+        for name, value in zip(("lre_grad", "lim_grad", "lst_grad"), made):
+            r_[name][one, :] = value
+
+    def store_rest(layer):
+        done = g_finish(2 * layer).astype(F32)
+        coef = (coef_all[0][layer:layer + 1], coef_all[1][layer:layer + 1])
+        turned = cmul(coef, (done[:, 0:state], done[:, state:2 * state]))
+        r_["c_grad"][layer, :, 0:state] = turned[0]
+        r_["c_grad"][layer, :, state:2 * state] = -turned[1]
+        r_["glu_grad"][layer] = done[:, 2 * state:]
+
+    store_small(1)
+    store_rest(1)
+    r_["b_grad"][1] = g_finish(3).astype(F32)
+    store_small(0)
+    store_rest(0)
+    r_["b_grad"][0] = g_finish(1).astype(F32)
+    for copy in unsent:
+        copy.wait_send()
+
+
+def run_main(planes, x_in, lengths, cotangent, norm_gain, lambda_re, lambda_im, log_step, skip_weight, glu_bias, weights):
+    depth = lax.axis_size("pipe")
     seqs, pos, model = x_in.shape
     layers, state = lambda_re.shape
     rows = seqs * pos
-    wide = weights.shape[2]
+    wide = 4 * state + model
     vmem = pl.BlockSpec(memory_space=pltpu.VMEM)
     smem = pl.BlockSpec(memory_space=pltpu.SMEM)
+    ins = dict(x=x_in, cot=cotangent, len=lengths, gain=norm_gain, lre=lambda_re, lim=lambda_im, lst=log_step,
+               skip=skip_weight, bias=glu_bias)
+    ins.update(zip(("b", "c", "glu") if planes else ("w",), weights))
+    outs = dict(out=(x_in.shape, BF16), xg=(x_in.shape, BF16))
+    scratch = dict(
+        h=pltpu.VMEM((layers + 1, rows, model), BF16),
+        go=pltpu.VMEM((rows, model), BF16),
+        xhat=pltpu.VMEM((layers, rows, model), F32),
+        rstd=pltpu.VMEM((layers, rows, 128), F32),
+        normed=pltpu.VMEM((layers, rows, model), BF16),
+        p=pltpu.VMEM((layers, rows, 2 * state), F32),
+        z=pltpu.VMEM((layers, rows + seqs * CHUNKS, 2 * state), F32),
+        zb=pltpu.VMEM((layers, rows, 2 * state), BF16),
+        dg=pltpu.VMEM((layers, rows, model), F32),
+        gated=pltpu.VMEM((layers, rows, model), BF16),
+        sig=pltpu.VMEM((layers, rows, model), F32),
+        gg=pltpu.VMEM((rows, model), BF16),
+        gb=pltpu.VMEM((rows, model), BF16),
+        gp=pltpu.VMEM((rows, 2 * state), BF16),
+        src=pltpu.VMEM((rows, 2 * state), F32),
+        tmp=pltpu.VMEM((rows, model), F32),
+        acc=pltpu.VMEM((rows, model), F32),
+        ends=pltpu.VMEM((2 * layers, 8, 2 * state), F32),
+        got=pltpu.VMEM((2 * layers, depth - 1, 8, 2 * state), F32),
+        send=pltpu.SemaphoreType.DMA((2 * layers, depth - 1)),
+        recv=pltpu.SemaphoreType.DMA((2 * layers, depth - 1)),
+    )
+    if planes:
+        local = weights[0].shape[1]
+        part = local // depth
+        full, halves = (layers, model), (layers, state)
+        outs.update(
+            gain_grad=(full, F32), lre_grad=(halves, F32), lim_grad=(halves, F32), lst_grad=(halves, F32),
+            b_grad=((layers, local, 2 * state), F32), c_grad=((layers, local, 2 * state), F32),
+            skip_grad=(full, F32), glu_grad=((layers, local, model), F32), bias_grad=(full, F32),
+        )
+        scratch.update(
+            small=pltpu.VMEM((layers, 8, model), F32),
+            s_other=pltpu.VMEM((layers, 8, model), F32),
+            s_quad=pltpu.VMEM((layers, depth, 8, model), F32),
+            s_line=pltpu.VMEM((layers, planes, 8, model), F32),
+            w=pltpu.VMEM((layers, planes, 2, depth, part, wide), BF16),
+        )
+        for kind, width in enumerate((2 * state + model, 2 * state)):
+            scratch.update({
+                f"part{kind}": pltpu.VMEM((layers, planes, 2, depth, part, width), BF16),
+                f"other{kind}": pltpu.VMEM((layers, planes, depth, part, width), BF16),
+                f"pair{kind}": pltpu.VMEM((layers, depth, planes, part, width), BF16),
+                f"quad{kind}": pltpu.VMEM((layers, depth - 1, planes, part, width), BF16),
+                f"line{kind}": pltpu.VMEM((layers, planes, part, width), BF16),
+                f"came{kind}": pltpu.VMEM((layers, planes - 1, part, width), BF16),
+                f"done{kind}": pltpu.VMEM((layers, depth, part, width), BF16),
+            })
+        for name, shape in dict(
+            w=(3, planes * depth), g=(2 * layers, 2 * depth + planes - 2), s=(layers, depth + planes - 1)
+        ).items():
+            scratch[name + "_send"] = pltpu.SemaphoreType.DMA(shape)
+            scratch[name + "_recv"] = pltpu.SemaphoreType.DMA(shape)
+    else:
+        outs.update(gpart=((layers, model, wide), F32), small=((layers, 8, model), F32))
+    names = tuple(ins) + tuple(outs) + tuple(scratch)
     return pl.pallas_call(
-        functools.partial(main_kernel, depth),
-        out_shape=(
-            jax.ShapeDtypeStruct(x_in.shape, BF16),
-            jax.ShapeDtypeStruct(x_in.shape, BF16),
-            jax.ShapeDtypeStruct((layers, model, wide), F32),
-            jax.ShapeDtypeStruct((layers, 8, model), F32),
-        ),
-        in_specs=[vmem, vmem, smem] + [vmem] * 7,
-        out_specs=(vmem,) * 4,
-        scratch_shapes=[
-            pltpu.VMEM((layers + 1, rows, model), BF16),
-            pltpu.VMEM((rows, model), BF16),
-            pltpu.VMEM((layers, rows, model), F32),
-            pltpu.VMEM((layers, rows, 128), F32),
-            pltpu.VMEM((layers, rows, model), BF16),
-            pltpu.VMEM((layers, rows, 2 * state), F32),
-            pltpu.VMEM((layers, rows + seqs * CHUNKS, 2 * state), F32),
-            pltpu.VMEM((layers, rows, 2 * state), BF16),
-            pltpu.VMEM((layers, rows, model), F32),
-            pltpu.VMEM((layers, rows, model), BF16),
-            pltpu.VMEM((layers, rows, model), F32),
-            pltpu.VMEM((rows, model), BF16),
-            pltpu.VMEM((rows, model), BF16),
-            pltpu.VMEM((rows, 2 * state), BF16),
-            pltpu.VMEM((rows, 2 * state), F32),
-            pltpu.VMEM((rows, model), F32),
-            pltpu.VMEM((rows, model), F32),
-            pltpu.VMEM((2 * layers, 8, 2 * state), F32),
-            pltpu.VMEM((2 * layers, depth - 1, 8, 2 * state), F32),
-            pltpu.SemaphoreType.DMA((2 * layers, depth - 1)),
-            pltpu.SemaphoreType.DMA((2 * layers, depth - 1)),
-        ],
+        functools.partial(main_kernel, depth, planes, names),
+        out_shape=tuple(jax.ShapeDtypeStruct(*o) for o in outs.values()),
+        in_specs=[smem if name == "len" else vmem for name in ins],
+        out_specs=(vmem,) * len(outs),
+        scratch_shapes=list(scratch.values()),
         compiler_params=pltpu.CompilerParams(
             collective_id=0, has_side_effects=True, vmem_limit_bytes=60 * 2**20
         ),
-    )(x_in, cotangent, lengths, norm_gain, lambda_re, lambda_im, log_step, skip_weight, glu_bias, weights)
+    )(*ins.values())
 
 
 def per_device(
     x_in, lengths, cotangent, norm_gain, lambda_re, lambda_im, log_step,
     b_weight, c_weight, skip_weight, glu_weight, glu_bias,
 ):
-    depth = lax.axis_size("pipe")
+    depth, owners = lax.axis_size("pipe"), lax.axis_size("dp")
     state = lambda_re.shape[1]
+    rest = (lambda_re, lambda_im, log_step, skip_weight, glu_bias)
+    if b_weight.shape[1] % (16 * depth) == 0 and owners % 2 == 0:
+        return run_main(owners // 2, x_in, lengths, cotangent, norm_gain, *rest, (b_weight, c_weight, glu_weight))
     _, _, coef = discretize(lambda_re, lambda_im, log_step)
     c_real, c_imag = c_weight[:, :, :state], c_weight[:, :, state:]
     turned = cmul((coef[0][:, None], coef[1][:, None]), (c_real, c_imag))
     shard = jnp.concatenate([b_weight, turned[0], -turned[1], glu_weight], axis=2).astype(BF16)
     weights = lax.all_gather(shard, "dp", axis=1, tiled=True)
     output, x_grad, gpart, small = run_main(
-        depth, x_in, lengths, cotangent, norm_gain, lambda_re, lambda_im, log_step, weights, skip_weight, glu_bias
+        0, x_in, lengths, cotangent, norm_gain, *rest, (weights,)
     )
     grads = lax.psum_scatter(gpart, "dp", scatter_dimension=1, tiled=True)
     grads = lax.psum(grads.astype(BF16), "pipe").astype(F32)

time: 259 us -> 101 us (0.39)
  waiting for transfers between devices: 140 us -> 0 us
  Pallas kernels: 48.5 us -> 90.8 us
  blocking collectives: 39.6 us -> 0 us
  between operations: 13.8 us -> 0.68 us
  other arithmetic: 10.1 us -> 0 us
    all_gather x1 -> x0, waiting for transfers between devices: 50 us -> none  [per_device(): weights = lax.all_gather(shard, 'dp', axis=1, tiled=True)]
    reduce_scatter x1 -> x0, waiting for transfers between devices: 47.4 us -> none  [per_device(): grads = lax.psum_scatter(gpart, 'dp', scatter_dimension=1, tiled=True)]
    psum x1 -> x0, waiting for transfers between devices: 42.7 us -> none  [per_device(): grads = lax.psum(grads.astype(BF16), 'pipe').astype(F32)]
    pallas_call x1, Pallas kernels: 48.5 us -> 90.8 us  [run_main(): pl.pallas_call(functools.partial(main_kernel, depth, planes, names), out_...]
    psum x1 -> x0, blocking collectives: 39.6 us -> none  [per_device(): small = lax.psum(small, ('pipe', 'dp'))]
    unnamed x16 -> x31, local copies, waits for them, and re-layouts: 3.46 us -> 9.12 us
    slice x4 -> x0, local copies, waits for them, and re-layouts: 3.35 us -> none  [the longest x1 1.7 us: per_device(): grads[:, :, :2 * state]]
    convert_element_type x2 -> x0, other arithmetic: 3.22 us -> none  [per_device(): grads = lax.psum(grads.astype(BF16), 'pipe').astype(F32)]
  transfers between devices with their start and end apart: 3 -> 0, of which waited for: 3 -> 0; matrix products, arithmetic and copies ran while one was open for 1% -> 0% of each run, Pallas kernels for 0% -> 0%
where the time goes in v2:
time: 101 us
  Pallas kernels  90.8 us (90%)
  local copies, waits for them, and re-layouts  9.12 us (9%)
    pallas_call x1, Pallas kernels, run_main(): pl.pallas_call(functools.partial(main_kernel, depth, planes, names), out_...  90.8 us
    unnamed x31, local copies, waits for them, and re-layouts  9.12 us

profile of v2, /device:TPU:0, one launch (start us, length us, event | category | flops | bytes accessed | tf_op | source)
XLA Modules:
  0.0 100.6 jit_solution(10844009895199207976)
XLA Ops:
  0.6 90.8 %shard_map.203 = (bf16[2,256,512]{2,1,0:T(8,128)(2,1)}, bf16[2,256,512]{2,1,0:T(8,128)(2,1)}, f32[2,512]{1,0:T(2,128)}, f32[2,384]{1,0:T(2,128)}, f32[2,384]{1,0...) custom-call(bf16[2,256,512]{2,1,0:T(8,128)(2,1)} %refs_0_.1, ...), custom_call_target="tpu_custom_call" | custom-call | tf_op jit(solution)/shard_map/pallas_call | solution.py:704
  91.5 0.0 copy-start
  91.5 1.9 %copy.34 = bf16[2,256,512]{2,1,0:T(8,128)(2,1)} copy(bf16[2,256,512]{2,1,0:T(8,128)(2,1)} %get-tuple-element.22) | data formatting | bytes 1048576
  93.4 0.0 copy-done
  93.4 0.0 copy-start.6
  93.4 0.8 copy.35
  94.2 0.0 copy-done.6
  94.2 0.6 copy.36
  94.8 0.1 copy-done.9
  94.9 0.6 copy.37
  95.5 0.1 copy-done.8
  95.6 0.6 copy.38
  96.1 0.1 copy-done.7
  96.2 0.6 copy.39
  96.8 0.0 copy-done.2
  96.8 0.7 copy.40
  97.6 0.4 copy-done.1
  98.0 0.7 copy.41
  98.7 0.0 copy-done.5
  98.7 0.6 copy.42
  99.3 0.0 copy-done.3
  99.3 0.7 copy.43
  100.0 0.0 copy-done.4
  100.0 0.6 copy.44
  (8 shorter events, 0.0 us)
Async XLA Ops:
  91.5 1.9 %copy-start = (bf16[2,256,512]{2,1,0:T(8,128)(2,1)S(1)}, bf16[2,256,512]{2,1,0:T(8,128)(2,1)}, u32[]{:S(2)}) copy-start(bf16[2,256,512]{2,1,0:T(8,128)(2,1)} %get-tuple-element.23) | copy-start | bytes 1572868
  93.4 0.8 copy-start.6
  93.4 3.4 %copy-start.2 = (f32[2,64,768]{2,1,0:T(8,128)S(1)}, f32[2,64,768]{2,1,0:T(8,128)}, u32[]{:S(2)}) copy-start(f32[2,64,768]{2,1,0:T(8,128)} %get-tuple-element.28) | copy-start | bytes 1179652
  94.2 0.7 copy-start.9
  94.9 0.7 copy-start.8
  95.6 0.7 copy-start.7
  96.8 1.1 %copy-start.1 = (f32[2,64,768]{2,1,0:T(8,128)S(1)}, f32[2,64,768]{2,1,0:T(8,128)}, u32[]{:S(2)}) copy-start(f32[2,64,768]{2,1,0:T(8,128)} %get-tuple-element.29) | copy-start | bytes 1179652
  98.0 0.8 copy-start.5
  98.0 1.3 %copy-start.3 = (f32[2,64,512]{2,1,0:T(8,128)S(1)}, f32[2,64,512]{2,1,0:T(8,128)}, u32[]{:S(2)}) copy-start(f32[2,64,512]{2,1,0:T(8,128)} %get-tuple-element.31) | copy-start | bytes 786436
  99.3 0.7 copy-start.4

commit v3 on v2

--- a/solution.py
+++ b/solution.py
@@ -10,6 +10,8 @@
 EPSILON = 1e-05
 CHUNKS = 8
 TILE = 32
+G1, C1, B1, G0, C0, B0 = range(6)
+GRAD_ORDERS = (True, False, False, True, False, False)
 MESH = pl.DeviceIdType.MESH
 F32 = jnp.float32
 BF16 = jnp.bfloat16
@@ -95,72 +97,75 @@
     return send, relay, swap, ready
 
 
-def gradient_sums(refs, kinds, depth, planes, me, plane, core, at_pipe, at_plane, at_core, remote):
+def gradient_sums(refs, orders, depth, planes, me, plane, core, at_pipe, at_plane, at_core, remote):
     sems = (refs["g_send"], refs["g_recv"])
     copies = {}
-
-    def of(name, piece):
-        return refs[name + str(piece % kinds)].at[piece // kinds]
-
-    def stage(piece, matrix, low, high):
-        part = of("part", piece)
-        part[..., low:high] = matrix.astype(BF16).reshape(part.shape[:-1] + (high - low,))
-
-    def start(piece):
-        part, other = of("part", piece), of("other", piece)
+    pipe_axis, plane_axis = (depth, me, at_pipe), (planes, plane, at_plane)
+
+    def axes(piece):
+        return (plane_axis, pipe_axis) if orders[piece] else (pipe_axis, plane_axis)
+
+    def start(piece, matrix):
+        part, other = refs[f"part{piece}"], refs[f"other{piece}"]
+        part[...] = matrix.astype(BF16).reshape(part.shape)
         copies[piece, 0] = remote(part.at[:, 1 - core], other, sems, (piece, 0), at_core)
 
-    def to_pipe(piece):
+    def first(piece):
         copies[piece, 0].wait_recv()
-        part, other, pair = of("part", piece), of("other", piece), of("pair", piece)
+        part, other, pair, quad = (refs[f"{name}{piece}"] for name in ("part", "other", "pair", "quad"))
 
         def add(i, carry):
             z, j = lax.div(i, depth), lax.rem(i, depth)
-            pair[j, z] = (part[z, core, j].astype(F32) + other[z, j].astype(F32)).astype(BF16)
+            total = (part[z, core, j].astype(F32) + other[z, j].astype(F32)).astype(BF16)
+            if orders[piece]:
+                pair[z, j] = total
+            else:
+                pair[j, z] = total
             return carry
-        lax.fori_loop(0, planes * depth, add, 0)
+        lax.fori_loop(0, planes * depth, add, 0, unroll=4)
+        count, here, there = axes(piece)[0]
         copies[piece, 1] = [
-            remote(pair.at[lax.rem(me + k, depth)], of("quad", piece).at[k - 1], sems, (piece, k), at_pipe(k))
-            for k in range(1, depth)
+            remote(pair.at[lax.rem(here + k, count)], quad.at[k - 1], sems, (piece, k), there(k)) for k in range(1, count)
         ]
 
-    def to_plane(piece):
-        pair, quad, line = of("pair", piece), of("quad", piece), of("line", piece)
+    def second(piece):
+        pair, quad, line, came = (refs[f"{name}{piece}"] for name in ("pair", "quad", "line", "came"))
         for copy in copies[piece, 1]:
             copy.wait_recv()
-
-        def add(z, carry):
-            total = pair[me, z].astype(F32)
-            for k in range(1, depth):
-                total = total + quad[k - 1, z].astype(F32)
-            line[z] = total.astype(BF16)
+        (count, here, _), (wide, there, go) = axes(piece)
+
+        def add(i, carry):
+            total = pair[here, i].astype(F32)
+            for k in range(1, count):
+                total = total + quad[k - 1, i].astype(F32)
+            line[i] = total.astype(BF16)
             return carry
-        lax.fori_loop(0, planes, add, 0)
+        lax.fori_loop(0, wide, add, 0, unroll=2)
         copies[piece, 2] = [
-            remote(line.at[lax.rem(plane + k, planes)], of("came", piece).at[k - 1], sems, (piece, depth + k - 1), at_plane(k))
-            for k in range(1, planes)
+            remote(line.at[lax.rem(there + k, wide)], came.at[k - 1], sems, (piece, count - 1 + k), go(k))
+            for k in range(1, wide)
         ]
 
-    def to_peers(piece):
-        line, came, done = of("line", piece), of("came", piece), of("done", piece)
+    def third(piece):
+        line, came, done = (refs[f"{name}{piece}"] for name in ("line", "came", "done"))
         for copy in copies[piece, 2]:
             copy.wait_recv()
-        total = line[plane].astype(F32)
-        for k in range(1, planes):
+        wide, there, _ = axes(piece)[1]
+        total = line[there].astype(F32)
+        for k in range(1, wide):
             total = total + came[k - 1].astype(F32)
         done[me] = total.astype(BF16)
         copies[piece, 3] = [
-            remote(done.at[me], done.at[me], sems, (piece, depth + planes + k - 2), at_pipe(k))
-            for k in range(1, depth)
+            remote(done.at[me], done.at[me], sems, (piece, depth + planes + k - 2), at_pipe(k)) for k in range(1, depth)
         ]
 
     def finish(piece):
         for copy in copies[piece, 3]:
             copy.wait_recv()
-        done = of("done", piece)[...]
-        return done.reshape(done.shape[0] * done.shape[1], done.shape[2])
-
-    return stage, start, to_pipe, to_plane, to_peers, finish
+        done = refs[f"done{piece}"][...]
+        return done.reshape(done.shape[0] * done.shape[1], done.shape[2]).astype(F32)
+
+    return start, first, second, third, finish
 
 
 def small_sums(refs, depth, planes, me, plane, core, at_pipe, at_plane, at_core, remote):
@@ -205,7 +210,7 @@
     r_ = dict(zip(names, refs))
     x_ref, cot_ref, len_ref, gain_ref = r_["x"], r_["cot"], r_["len"], r_["gain"]
     lre_ref, lim_ref, lst_ref, skip_ref, bias_ref = r_["lre"], r_["lim"], r_["lst"], r_["skip"], r_["bias"]
-    out_ref, xg_ref, small_ref = r_["out"], r_["xg"], r_["small"]
+    small_ref = r_["small"]
     h_ref, go_ref, xhat_ref, rstd_ref, normed_ref = r_["h"], r_["go"], r_["xhat"], r_["rstd"], r_["normed"]
     p_ref, z_ref, zb_ref, dg_ref, gated_ref, sig_ref = r_["p"], r_["z"], r_["zb"], r_["dg"], r_["gated"], r_["sig"]
     gg_ref, gb_ref, gp_ref, src_ref, tmp_ref, acc_ref = r_["gg"], r_["gb"], r_["gp"], r_["src"], r_["tmp"], r_["acc"]
@@ -261,9 +266,9 @@
             return body(pl.ds(pl.multiple_of(q * pos + i * TILE, TILE), TILE), masks[q], carry)
         return lax.fori_loop(0, pos // TILE, step, init, unroll=unroll)
 
-    def all_tiles(body, init=0):
+    def all_tiles(body, init=0, unroll=2):
         for q in range(seqs):
-            init = tiles(body, q, init)
+            init = tiles(body, q, init, unroll)
         return init
 
     def fold(value):
@@ -272,30 +277,44 @@
             total = total + value[r:r + 8]
         return total
 
+    fetches = {}
+    for at, name in enumerate(("b", "x", "c", "glu", "cot") if planes else ("x", "cot")):
+        fetches[name] = pltpu.make_async_copy(r_[name], r_[name + "_here"], r_["fetch"].at[at])
+        fetches[name].start()
+    x_here, cot_here = r_["x_here"], r_["cot_here"]
     step_all, decay_all, coef_all = discretize(lre_ref[...], lim_ref[...], lst_ref[...])
     if planes:
         ways = (depth, planes, me, plane, core, at_pipe, at_plane, at_core, remote)
-        pieces = ((0, 0, 2 * state), (0, 2 * state, 4 * state + model), (1, 0, 4 * state + model))
+        wide = 4 * state + model
+        pieces = ((0, 0, 2 * state), (0, 2 * state, wide), (1, 0, 2 * state), (1, 2 * state, wide))
         w_send, w_relay, w_swap, w_ready = weight_gather(r_, pieces, *ways)
-        g_stage, g_start, g_pipe, g_plane, g_peers, g_finish = gradient_sums(r_, 2, *ways)
+        g_start, g_first, g_second, g_third, g_finish = gradient_sums(r_, GRAD_ORDERS, *ways)
         s_start, s_pipe, s_plane, s_finish = small_sums(r_, *ways)
+
+        def keep(layer, matrix, low):
+            high = low + matrix.shape[1]
+            w_ref[layer, plane, core, :, :, low:high] = matrix.astype(BF16).reshape(depth, -1, high - low)
+
+        fetches["b"].wait()
         for layer in range(layers):
-            own = w_ref.at[layer, plane, core]
-
-            def keep(matrix, low):
-                high = low + matrix.shape[1]
-                own[:, :, low:high] = matrix.astype(BF16).reshape(depth, matrix.shape[0] // depth, high - low)
-            keep(r_["b"][layer], 0)
-            coef = (coef_all[0][layer:layer + 1], coef_all[1][layer:layer + 1])
-            turned = cmul(coef, (r_["c"][layer, :, 0:state], r_["c"][layer, :, state:2 * state]))
-            keep(turned[0], 2 * state)
-            keep(-turned[1], 3 * state)
-            keep(r_["glu"][layer], 4 * state)
+            keep(layer, r_["b_here"][layer], 0)
     pl.semaphore_wait(barrier, len(others))
     if planes:
         w_send(0)
+        fetches["c"].wait()
+        fetches["glu"].wait()
+        for layer in range(layers):
+            coef = (coef_all[0][layer:layer + 1], coef_all[1][layer:layer + 1])
+            turned = cmul(coef, (r_["c_here"][layer, :, 0:state], r_["c_here"][layer, :, state:2 * state]))
+            keep(layer, turned[0], 2 * state)
+            keep(layer, -turned[1], 3 * state)
+            keep(layer, r_["glu_here"][layer], 4 * state)
+        w_send(1)
+        w_send(2)
+        w_send(3)
+    fetches["x"].wait()
     for q in range(seqs):
-        h_ref[0, seq_rows(q), :] = dot(spread, x_ref[q], NN).astype(BF16)
+        h_ref[0, seq_rows(q), :] = dot(spread, x_here[q], NN).astype(BF16)
 
     def matrix(layer, which):
         low, high = (0, 2 * state, 4 * state)[which], (2 * state, 4 * state, w_ref.shape[-1])[which]
@@ -329,55 +348,67 @@
             value = cmul(value, value)
         return value
 
-    def start_exchange(number, ends, decay, down):
-        power = squared(decay, steps.bit_length() - 1)
-        jump, before = power, []
+    lanes = 128
+    spans = state // lanes
+
+    def chunk_powers(layer):
+        powers = [squared(wide_decay(layer), steps.bit_length() - 1)]
+        while len(powers) < CHUNKS.bit_length():
+            powers.append(cmul(powers[-1], powers[-1]))
+        return powers
+
+    def place_table(powers, down):
+        place = (CHUNKS - 1 - sublane) if down else sublane
+        table = (jnp.ones((CHUNKS, state), F32), zero)
+        for bit, factor in enumerate(powers[:-1]):
+            moved = cmul(table, factor)
+            take = lax.rem(lax.div(place, 1 << bit), 2) == 1
+            table = (jnp.where(take, moved[0], table[0]), jnp.where(take, moved[1], table[1]))
+        return table
+
+    def start_exchange(number, ends, powers, down):
         sums = list(ends)
-        k = 1
-        while k < CHUNKS:
+        for bit, jump in enumerate(powers[:-1]):
             for q in range(seqs):
-                moved = cmul(jump, (shifted(sums[q][0], k, down), shifted(sums[q][1], k, down)))
+                moved = cmul(jump, (shifted(sums[q][0], 1 << bit, down), shifted(sums[q][1], 1 << bit, down)))
                 sums[q] = (sums[q][0] + moved[0], sums[q][1] + moved[1])
-            before.append(jump)
-            jump = cmul(jump, jump)
-            k *= 2
         last = 0 if down else CHUNKS - 1
         for q in range(seqs):
-            ends_ref[number, q:q + 1, 0:state] = sums[q][0][last:last + 1]
-            ends_ref[number, q:q + 1, state:2 * state] = sums[q][1][last:last + 1]
+            for part in range(2):
+                for j in range(spans):
+                    at = (q * 2 + part) * spans + j
+                    ends_ref[number, at:at + 1, :] = sums[q][part][last:last + 1, j * lanes:(j + 1) * lanes]
         copies = [
             remote(ends_ref.at[number], got_ref.at[number, k - 1], (send_sems, recv_sems), (number, k - 1),
                    at_pipe(depth - k if down else k))
             for k in range(1, depth)
         ]
-        place = (CHUNKS - 1 - sublane) if down else sublane
-        table = (jnp.ones((CHUNKS, state), F32), zero)
-        for bit, factor in enumerate(before):
-            moved = cmul(table, factor)
-            take = lax.rem(lax.div(place, 1 << bit), 2) == 1
-            table = (jnp.where(take, moved[0], table[0]), jnp.where(take, moved[1], table[1]))
+        return copies, sums
+
+    def finish_exchange(number, pending, powers, down):
+        copies, sums = pending
+        table = place_table(powers, down)
         exclusive = [(shifted(s[0], 1, down), shifted(s[1], 1, down)) for s in sums]
-        return copies, jump, table, exclusive
-
-    def finish_exchange(number, pending, down):
-        copies, jump, table, exclusive = pending
         for copy in copies:
             copy.wait_recv()
-        jump_row = (jump[0][0:1], jump[1][0:1])
+        jump = powers[-1]
         carries = []
         for q in range(seqs):
-            total = (jnp.zeros((1, state), F32), jnp.zeros((1, state), F32))
-            factor = (jnp.ones((1, state), F32), jnp.zeros((1, state), F32))
+            total, factor = (zero, zero), (jnp.ones((CHUNKS, state), F32), zero)
             for k in range(1, depth):
-                there = (me + k < depth) if down else (me - k >= 0)
-                there = there.astype(F32)
-                came = got_ref[number, k - 1]
-                came = (came[q:q + 1, 0:state] * there, came[q:q + 1, state:2 * state] * there)
+                there = ((me + k < depth) if down else (me - k >= 0)).astype(F32)
+                came = []
+                for part in range(2):
+                    at = (q * 2 + part) * spans
+                    pieces_ = [
+                        jnp.broadcast_to(got_ref[number, k - 1, at + j:at + j + 1, :], (CHUNKS, lanes))
+                        for j in range(spans)
+                    ]
+                    came.append(jnp.concatenate(pieces_, axis=1) * there)
                 moved = cmul(factor, came)
                 total = (total[0] + moved[0], total[1] + moved[1])
-                factor = cmul(factor, jump_row)
-            wide = (jnp.broadcast_to(total[0], (CHUNKS, state)), jnp.broadcast_to(total[1], (CHUNKS, state)))
-            moved = cmul(table, wide)
+                factor = cmul(factor, jump)
+            moved = cmul(table, total)
             carries.append((exclusive[q][0] + moved[0], exclusive[q][1] + moved[1]))
         return carries
 
@@ -385,6 +416,10 @@
         return tuple(jnp.broadcast_to(part[layer:layer + 1], (CHUNKS, state)) for part in decay_all)
 
     small_ref[...] = jnp.zeros_like(small_ref)
+    powers_of = [chunk_powers(layer) for layer in range(layers)]
+
+    def back_powers(layer):
+        return [conj(power) for power in powers_of[layer]]
 
     for layer in range(layers):
         down = layer % 2 == 1
@@ -404,29 +439,30 @@
             rstd_ref[layer, r, :] = jnp.broadcast_to(rstd, (TILE, 128))
             normed_ref[layer, r, :] = (xhat * gain * mask).astype(BF16)
             return carry
-        all_tiles(norm_tile)
-
+        all_tiles(norm_tile, unroll=4)
+
+        if layer == 0:
+            if planes:
+                w_relay(0)
+            fetches["cot"].wait()
+            for q in range(seqs):
+                go_ref[seq_rows(q), :] = dot(spread, cot_here[q], NN).astype(BF16)
         if planes and layer == 0:
-            w_relay(0)
-            w_send(1)
-        if layer == 0:
-            for q in range(seqs):
-                go_ref[seq_rows(q), :] = dot(spread, cot_ref[q], NN).astype(BF16)
-        if planes and layer == 0:
+            w_relay(1)
             w_swap(0)
-            w_relay(1)
-            w_send(2)
             w_ready(0)
         if planes and layer == 1:
-            w_swap(2)
             w_ready(2)
-
         p_ref[layer] = dot(normed_ref[layer], matrix(layer, 0), NN)
         ends = scan_ends(p_ref.at[layer], decay, down)
-        pending = start_exchange(layer, ends, decay, down)
+        pending = start_exchange(layer, ends, powers_of[layer], down)
         if planes and layer == 0:
             w_relay(2)
-        carries = finish_exchange(layer, pending, down)
+            w_relay(3)
+            w_swap(1)
+        if planes and layer == 1:
+            w_swap(3)
+        carries = finish_exchange(layer, pending, powers_of[layer], down)
         pad = pos + CHUNKS
         for q in range(seqs):
             at = q * pad + (pos if down else 0)
@@ -457,9 +493,8 @@
             return tuple(carry)
         lax.fori_loop(0, steps // 2, state_pair, tuple(carries), unroll=2)
 
-        if planes and layer == 0:
-            w_swap(1)
-            w_ready(1)
+        if planes:
+            w_ready(2 * layer + 1)
         tmp_ref[...] = dot(zb_ref[layer], matrix(layer, 1), NT)
 
         def gelu_tile(r, mask, carry):
@@ -478,11 +513,24 @@
             made = h_ref[layer, r, :].astype(F32) + mask * (gated_ref[layer, r, :].astype(F32) * sig)
             h_ref[layer + 1, r, :] = made.astype(BF16)
             return carry
+        if planes and layer == 0:
+            w_swap(2)
         all_tiles(out_tile)
+
+    puts = []
+
+    def put(name, at=None):
+        source, target = r_[name + "_here"], r_[name]
+        if at is not None:
+            source, target = source.at[at], target.at[at]
+        copy = pltpu.make_async_copy(source, target, r_["put"].at[len(puts)])
+        copy.start()
+        puts.append(copy)
 
     gather = (lax.rem(row, steps) * CHUNKS + lax.div(row, steps) == col).astype(F32).astype(BF16)
     for q in range(seqs):
-        out_ref[q] = dot(gather, h_ref[layers, seq_rows(q), :], NN).astype(BF16)
+        r_["out_here"][q] = dot(gather, h_ref[layers, seq_rows(q), :], NN).astype(BF16)
+    put("out")
 
     for layer in reversed(range(layers)):
         down = layer % 2 == 1
@@ -499,6 +547,8 @@
             acc_ref[r, :] = branch
             return carry + fold(grad.astype(F32))
         bias_sum = all_tiles(gate_tile, zero_row)
+        if planes and layer == 0:
+            g_start(G0, dot(gated_ref[layer], gg_ref[...], TN))
         tmp_ref[...] = dot(gg_ref[...], matrix(layer, 2), NT)
 
         def before_tile(r, mask, carry):
@@ -508,22 +558,28 @@
             return carry + fold(grad.astype(F32) * normed_ref[layer, r, :].astype(F32))
         skip_sum = all_tiles(before_tile, zero_row)
 
+        if planes and layer == 0:
+            g_first(G0)
         src_ref[...] = dot(gb_ref[...], matrix(layer, 1), NN)
         back = conj(decay)
         ends = scan_ends(src_ref, back, not down)
-        pending = start_exchange(layers + layer, ends, back, not down)
-        glu_part = dot(gated_ref[layer], gg_ref[...], TN)
+        pending = start_exchange(layers + layer, ends, back_powers(layer), not down)
+        if planes and layer == 0:
+            g_first(B1)
         c_part = dot(gb_ref[...], zb_ref[layer], TN)
-        if planes:
-            g_stage(2 * layer, c_part, 0, 2 * state)
-            g_stage(2 * layer, glu_part, 2 * state, 2 * state + model)
-            g_start(2 * layer)
-            if layer == 0:
-                g_plane(2)
+        if not planes:
+            r_["gpart"][layer, :, 4 * state:] = dot(gated_ref[layer], gg_ref[...], TN)
+            r_["gpart"][layer, :, 2 * state:4 * state] = c_part
+        elif layer == 1:
+            g_start(C1, c_part)
+            g_start(G1, dot(gated_ref[layer], gg_ref[...], TN))
+            g_first(C1)
         else:
-            r_["gpart"][layer, :, 4 * state:] = glu_part
-            r_["gpart"][layer, :, 2 * state:4 * state] = c_part
-        carries = finish_exchange(layers + layer, pending, not down)
+            g_start(C0, c_part)
+            g_second(C1)
+            s_pipe(1)
+            g_first(C0)
+        carries = finish_exchange(layers + layer, pending, back_powers(layer), not down)
 
         def adjoint_pair(i, loop):
             carry, sums = list(loop[0]), list(loop[1])
@@ -555,16 +611,17 @@
         _, sums = lax.fori_loop(0, steps // 2, adjoint_pair, (tuple(carries), (zero,) * 4), unroll=1)
 
         b_part = dot(normed_ref[layer], gp_ref[...], TN)
-        if planes:
-            g_stage(2 * layer + 1, b_part, 0, 2 * state)
-            g_start(2 * layer + 1)
-            g_pipe(2 * layer)
-            if layer == 0:
-                g_plane(3)
-                g_peers(2)
+        if not planes:
+            r_["gpart"][layer, :, 0:2 * state] = b_part
+        elif layer == 1:
+            g_start(B1, b_part)
+            g_first(G1)
         else:
-            r_["gpart"][layer, :, 0:2 * state] = b_part
+            g_start(B0, b_part)
         tmp_ref[...] = dot(gp_ref[...], matrix(layer, 0), NT)
+        if planes and layer == 0:
+            g_first(B0)
+            g_second(G1)
 
         def input_tile(r, mask, carry):
             grad = (tmp_ref[r, :] + skip * gb_ref[r, :].astype(F32)) * mask
@@ -576,7 +633,7 @@
             made = go_ref[r, :].astype(F32) + rstd * (scaled - first - xhat * second)
             go_ref[r, :] = made.astype(BF16)
             return carry + fold(grad * xhat)
-        gain_sum = all_tiles(input_tile, zero_row)
+        gain_sum = all_tiles(input_tile, zero_row, unroll=4)
 
         for at, value in enumerate((gain_sum, skip_sum, bias_sum)):
             small_ref[layer, at:at + 1, :] = jnp.sum(value, axis=0, keepdims=True)
@@ -584,52 +641,91 @@
             small_ref[layer, 3 + at:4 + at, 0:state] = jnp.sum(value, axis=0, keepdims=True)
         if planes:
             s_start(layer)
-            g_pipe(2 * layer + 1)
-            s_pipe(layer)
 
     for q in range(seqs):
-        xg_ref[q] = dot(gather, go_ref[seq_rows(q), :], NN).astype(BF16)
-    if not planes:
-        for copy in unsent:
-            copy.wait_send()
-        return
-    g_peers(3)
-    g_plane(0)
-    s_plane(1)
-    g_plane(1)
-    s_plane(0)
-    g_peers(0)
-    g_peers(1)
-
-    def store_small(layer):
-        total = s_finish(layer)
-        for at, name in enumerate(("gain_grad", "skip_grad", "bias_grad")):
-            r_[name][layer:layer + 1, :] = total[at:at + 1, :]
-        one = slice(layer, layer + 1)
-        coef = (coef_all[0][one], coef_all[1][one])
-        sums = [total[at:at + 1, 0:state] for at in range(3, 7)]
-        scale = coef[0] * coef[0] + coef[1] * coef[1]
-        coef_grad = cmul((sums[2], sums[3]), (coef[0] / scale, coef[1] / scale))
-        made = discretize_grads(lre_ref[one], lim_ref[one], lst_ref[one], (sums[0], sums[1]), coef_grad)
-        for name, value in zip(("lre_grad", "lim_grad", "lst_grad"), made):
-            r_[name][one, :] = value
-
-    def store_rest(layer):
-        done = g_finish(2 * layer).astype(F32)
-        coef = (coef_all[0][layer:layer + 1], coef_all[1][layer:layer + 1])
-        turned = cmul(coef, (done[:, 0:state], done[:, state:2 * state]))
-        r_["c_grad"][layer, :, 0:state] = turned[0]
-        r_["c_grad"][layer, :, state:2 * state] = -turned[1]
-        r_["glu_grad"][layer] = done[:, 2 * state:]
-
-    store_small(1)
-    store_rest(1)
-    r_["b_grad"][1] = g_finish(3).astype(F32)
-    store_small(0)
-    store_rest(0)
-    r_["b_grad"][0] = g_finish(1).astype(F32)
+        r_["xg_here"][q] = dot(gather, go_ref[seq_rows(q), :], NN).astype(BF16)
+    put("xg")
+    if planes:
+        def store_small(layer):
+            total = s_finish(layer)
+            for at, name in enumerate(("gain_grad", "skip_grad", "bias_grad")):
+                r_[name][layer:layer + 1, :] = total[at:at + 1, :]
+            one = slice(layer, layer + 1)
+            coef = (coef_all[0][one], coef_all[1][one])
+            sums = [total[at:at + 1, 0:state] for at in range(3, 7)]
+            scale = coef[0] * coef[0] + coef[1] * coef[1]
+            coef_grad = cmul((sums[2], sums[3]), (coef[0] / scale, coef[1] / scale))
+            made = discretize_grads(lre_ref[one], lim_ref[one], lst_ref[one], (sums[0], sums[1]), coef_grad)
+            for name, value in zip(("lre_grad", "lim_grad", "lst_grad"), made):
+                r_[name][one, :] = value
+
+        def store_b(layer, piece):
+            r_["b_grad_here"][layer] = g_finish(piece)
+            put("b_grad", layer)
+
+        def store_c(layer, piece):
+            coef = (coef_all[0][layer:layer + 1], coef_all[1][layer:layer + 1])
+            done = g_finish(piece)
+            turned = cmul(coef, (done[:, 0:state], done[:, state:2 * state]))
+            r_["c_grad_here"][layer, :, 0:state] = turned[0]
+            r_["c_grad_here"][layer, :, state:2 * state] = -turned[1]
+            put("c_grad", layer)
+
+        def store_glu(layer, piece):
+            r_["glu_grad_here"][layer] = g_finish(piece)
+            put("glu_grad", layer)
+
+        s_pipe(0)
+        s_plane(1)
+        g_second(B1)
+        g_third(C1)
+        g_second(G0)
+        g_second(C0)
+        g_third(G1)
+        g_second(B0)
+        s_plane(0)
+        g_third(B1)
+        g_third(G0)
+        store_small(1)
+        store_c(1, C1)
+        store_glu(1, G1)
+        g_third(C0)
+        store_b(1, B1)
+        g_third(B0)
+        store_small(0)
+        store_glu(0, G0)
+        store_c(0, C0)
+        store_b(0, B0)
+    for copy in puts:
+        copy.wait()
     for copy in unsent:
         copy.wait_send()
+
+
+def copy_kernel(*refs):
+    count = (len(refs) - 2) // 3
+    sources, targets, held, (in_sems, out_sems) = refs[:count], refs[count:2 * count], refs[2 * count:3 * count], refs[3 * count:]
+    arrive = [pltpu.make_async_copy(sources[i], held[i], in_sems.at[i]) for i in range(count)]
+    leave = [pltpu.make_async_copy(held[i], targets[i], out_sems.at[i]) for i in range(count)]
+    for copy in arrive:
+        copy.start()
+    for first, then in zip(arrive, leave):
+        first.wait()
+        then.start()
+    for copy in leave:
+        copy.wait()
+
+
+def copied(results):
+    anywhere = pl.BlockSpec(memory_space=pl.ANY)
+    return pl.pallas_call(
+        copy_kernel,
+        out_shape=tuple(jax.ShapeDtypeStruct(r.shape, r.dtype) for r in results),
+        in_specs=[anywhere] * len(results),
+        out_specs=(anywhere,) * len(results),
+        scratch_shapes=[pltpu.VMEM(r.shape, r.dtype) for r in results] + [pltpu.SemaphoreType.DMA((len(results),))] * 2,
+        compiler_params=pltpu.CompilerParams(vmem_limit_bytes=60 * 2**20),
+    )(*results)
 
 
 def run_main(planes, x_in, lengths, cotangent, norm_gain, lambda_re, lambda_im, log_step, skip_weight, glu_bias, weights):
@@ -638,8 +734,10 @@
     layers, state = lambda_re.shape
     rows = seqs * pos
     wide = 4 * state + model
+    message = -(-seqs * 2 * state // (8 * 128)) * 8
     vmem = pl.BlockSpec(memory_space=pltpu.VMEM)
     smem = pl.BlockSpec(memory_space=pltpu.SMEM)
+    anywhere = pl.BlockSpec(memory_space=pl.ANY)
     ins = dict(x=x_in, cot=cotangent, len=lengths, gain=norm_gain, lre=lambda_re, lim=lambda_im, lst=log_step,
                skip=skip_weight, bias=glu_bias)
     ins.update(zip(("b", "c", "glu") if planes else ("w",), weights))
@@ -662,8 +760,10 @@
         src=pltpu.VMEM((rows, 2 * state), F32),
         tmp=pltpu.VMEM((rows, model), F32),
         acc=pltpu.VMEM((rows, model), F32),
-        ends=pltpu.VMEM((2 * layers, 8, 2 * state), F32),
-        got=pltpu.VMEM((2 * layers, depth - 1, 8, 2 * state), F32),
+        ends=pltpu.VMEM((2 * layers, message, 128), F32),
+        got=pltpu.VMEM((2 * layers, depth - 1, message, 128), F32),
+        fetch=pltpu.SemaphoreType.DMA((5,)),
+        put=pltpu.SemaphoreType.DMA((8,)),
         send=pltpu.SemaphoreType.DMA((2 * layers, depth - 1)),
         recv=pltpu.SemaphoreType.DMA((2 * layers, depth - 1)),
     )
@@ -683,29 +783,37 @@
             s_line=pltpu.VMEM((layers, planes, 8, model), F32),
             w=pltpu.VMEM((layers, planes, 2, depth, part, wide), BF16),
         )
-        for kind, width in enumerate((2 * state + model, 2 * state)):
+        for piece, first_plane in enumerate(GRAD_ORDERS):
+            width = model if piece in (G0, G1) else 2 * state
+            count, other = (planes, depth) if first_plane else (depth, planes)
             scratch.update({
-                f"part{kind}": pltpu.VMEM((layers, planes, 2, depth, part, width), BF16),
-                f"other{kind}": pltpu.VMEM((layers, planes, depth, part, width), BF16),
-                f"pair{kind}": pltpu.VMEM((layers, depth, planes, part, width), BF16),
-                f"quad{kind}": pltpu.VMEM((layers, depth - 1, planes, part, width), BF16),
-                f"line{kind}": pltpu.VMEM((layers, planes, part, width), BF16),
-                f"came{kind}": pltpu.VMEM((layers, planes - 1, part, width), BF16),
-                f"done{kind}": pltpu.VMEM((layers, depth, part, width), BF16),
+                f"part{piece}": pltpu.VMEM((planes, 2, depth, part, width), BF16),
+                f"other{piece}": pltpu.VMEM((planes, depth, part, width), BF16),
+                f"pair{piece}": pltpu.VMEM((count, other, part, width), BF16),
+                f"quad{piece}": pltpu.VMEM((count - 1, other, part, width), BF16),
+                f"line{piece}": pltpu.VMEM((other, part, width), BF16),
+                f"came{piece}": pltpu.VMEM((other - 1, part, width), BF16),
+                f"done{piece}": pltpu.VMEM((depth, part, width), BF16),
             })
         for name, shape in dict(
-            w=(3, planes * depth), g=(2 * layers, 2 * depth + planes - 2), s=(layers, depth + planes - 1)
+            w=(4, planes * depth), g=(6, 2 * depth + planes - 2), s=(layers, depth + planes - 1)
         ).items():
             scratch[name + "_send"] = pltpu.SemaphoreType.DMA(shape)
             scratch[name + "_recv"] = pltpu.SemaphoreType.DMA(shape)
     else:
         outs.update(gpart=((layers, model, wide), F32), small=((layers, 8, model), F32))
+    fetched = ("x", "cot", "b", "c", "glu") if planes else ("x", "cot")
+    for name in fetched:
+        scratch[name + "_here"] = pltpu.VMEM(ins[name].shape, ins[name].dtype)
+    stored = ("out", "xg", "b_grad", "c_grad", "glu_grad") if planes else ("out", "xg")
+    for name in stored:
+        scratch[name + "_here"] = pltpu.VMEM(*outs[name])
     names = tuple(ins) + tuple(outs) + tuple(scratch)
     return pl.pallas_call(
         functools.partial(main_kernel, depth, planes, names),
         out_shape=tuple(jax.ShapeDtypeStruct(*o) for o in outs.values()),
-        in_specs=[smem if name == "len" else vmem for name in ins],
-        out_specs=(vmem,) * len(outs),
+        in_specs=[smem if name == "len" else anywhere if name in fetched else vmem for name in ins],
+        out_specs=tuple(anywhere if name in stored else vmem for name in outs),
         scratch_shapes=list(scratch.values()),
         compiler_params=pltpu.CompilerParams(
             collective_id=0, has_side_effects=True, vmem_limit_bytes=60 * 2**20
@@ -721,7 +829,7 @@
     state = lambda_re.shape[1]
     rest = (lambda_re, lambda_im, log_step, skip_weight, glu_bias)
     if b_weight.shape[1] % (16 * depth) == 0 and owners % 2 == 0:
-        return run_main(owners // 2, x_in, lengths, cotangent, norm_gain, *rest, (b_weight, c_weight, glu_weight))
+        return copied(run_main(owners // 2, x_in, lengths, cotangent, norm_gain, *rest, (b_weight, c_weight, glu_weight)))
     _, _, coef = discretize(lambda_re, lambda_im, log_step)
     c_real, c_imag = c_weight[:, :, :state], c_weight[:, :, state:]
     turned = cmul((coef[0][:, None], coef[1][:, None]), (c_real, c_imag))

time: 101 us -> 78.7 us (0.78)
  Pallas kernels: 90.8 us -> 77.9 us
  local copies, waits for them, and re-layouts: 9.12 us -> 0 us
    pallas_call x1, Pallas kernels: 90.8 us -> 75.3 us  [run_main(): pl.pallas_call(functools.partial(main_kernel, depth, planes, names), out_...]
    unnamed x31 -> x0, local copies, waits for them, and re-layouts: 9.12 us -> none
    pallas_call x0 -> x1, Pallas kernels: none -> 2.57 us  [copied(): pl.pallas_call(copy_kernel, out_shape=tuple((jax.ShapeDtypeStruct(r.shape...]
where the time goes in v3:
time: 78.7 us; the launch traced here: 78.5 us
  Pallas kernels  77.9 us (99%)
    pallas_call x1, Pallas kernels, run_main(): pl.pallas_call(functools.partial(main_kernel, depth, planes, names), out_...  75.3 us
    pallas_call x1, Pallas kernels, copied(): pl.pallas_call(copy_kernel, out_shape=tuple((jax.ShapeDtypeStruct(r.shape...  2.57 us

profile of v3, /device:TPU:0, one launch (start us, length us, event | category | flops | bytes accessed | tf_op | source)
XLA Modules:
  0.0 78.5 jit_solution(2703712389993086705)
XLA Ops:
  0.6 75.3 %shard_map.203 = (bf16[2,256,512]{2,1,0:T(8,128)(2,1)}, bf16[2,256,512]{2,1,0:T(8,128)(2,1)}, f32[2,512]{1,0:T(2,128)}, f32[2,384]{1,0:T(2,128)}, f32[2,384]{1,0...) custom-call(bf16[2,256,512]{2,1,0:T(8,128)(2,1)} %refs_0_.1, ...), custom_call_target="tpu_custom_call" | custom-call | tf_op jit(solution)/shard_map/pallas_call | solution.py:812
  76.0 2.6 %shard_map.204 = (bf16[2,256,512]{2,1,0:T(8,128)(2,1)}, bf16[2,256,512]{2,1,0:T(8,128)(2,1)}, f32[2,512]{1,0:T(2,128)}, f32[2,384]{1,0:T(2,128)}, f32[2,384]{1,0...) custom-call(bf16[2,256,512]{2,1,0:T(8,128)(2,1)} %get-tuple-element., ...), custom_call_target="tpu_custom_call" | custom-call | tf_op jit(solution)/shard_map/pallas_call | solution.py:721

commit v4 on v3

--- a/solution.py
+++ b/solution.py
@@ -9,15 +9,47 @@
 
 EPSILON = 1e-05
 CHUNKS = 8
-TILE = 32
-G1, C1, B1, G0, C0, B0 = range(6)
-GRAD_ORDERS = (True, False, False, True, False, False)
+TILE = 64
+X, COT, NORM, PROJ, ENDS, SCAN, CDOT, GELU, GDOT, OUT, RESULT, GATE, GBACK, BEFORE, SRC, BENDS, BSCAN, CGRAD, GGRAD, BGRAD, XDOT, BNORM, XG = range(23)
+FOLD, WSEND, WRELAY, WFORWARD, WSWAP, WREADY, FIRST, MIDDLE, SECOND, THIRD, FOURTH, SAVE, SSTART, SPIPE, SPLANE, SSAVE = range(23, 39)
+ORDER = (
+    (WSEND, 1), (X, 0), (WSEND, 0), (FOLD, 0), (FOLD, 1), (WSEND, 4), (WSEND, 3), (WRELAY, 1), (WRELAY, 0),
+    (WSEND, 2), (WRELAY, 4), (WSWAP, 1), (WSEND, 6), (WRELAY, 3), (WSWAP, 0), (WSEND, 5), (COT, 0), (WRELAY, 2),
+    (WFORWARD, 4), (WFORWARD, 3), (WREADY, 1), (WREADY, 0), (NORM, 0), (PROJ, 0), (ENDS, 0), (WFORWARD, 2),
+    (WSWAP, 4), (WRELAY, 5), (WSWAP, 3), (WREADY, 3), (WSWAP, 2), (WRELAY, 6), (WREADY, 4), (SCAN, 0), (WREADY, 2),
+    (CDOT, 0), (GELU, 0), (WFORWARD, 5), (GDOT, 0), (OUT, 0), (NORM, 1), (PROJ, 1), (ENDS, 1), (WSWAP, 5), (WSWAP, 6),
+    (WREADY, 6), (WREADY, 5), (SCAN, 1), (CDOT, 1), (GELU, 1), (GDOT, 1), (OUT, 1), (GATE, 1), (GBACK, 1),
+    (BEFORE, 1), (SRC, 1), (BENDS, 1), (CGRAD, 1), (GGRAD, 1), (FIRST, 0), (FIRST, 1), (BSCAN, 1), (XDOT, 1),
+    (BGRAD, 1), (BNORM, 1), (GATE, 0), (GGRAD, 0), (GBACK, 0), (MIDDLE, 0), (BEFORE, 0), (FIRST, 2), (CGRAD, 0),
+    (FIRST, 3), (SRC, 0), (BENDS, 0), (FIRST, 4), (SECOND, 0), (MIDDLE, 1), (MIDDLE, 2), (BSCAN, 0), (BGRAD, 0),
+    (SSTART, 1), (MIDDLE, 4), (SECOND, 1), (FIRST, 5), (FIRST, 6), (XDOT, 0), (SECOND, 2), (SECOND, 3), (BNORM, 0),
+    (SSTART, 0), (SECOND, 4), (SPIPE, 0), (THIRD, 1), (SPIPE, 1), (SECOND, 5), (THIRD, 0), (SECOND, 6), (THIRD, 2),
+    (THIRD, 3), (SPLANE, 0), (FOURTH, 1), (XG, 0), (THIRD, 4), (SPLANE, 1), (FOURTH, 0), (THIRD, 5), (FOURTH, 2),
+    (FOURTH, 3), (THIRD, 6), (FOURTH, 4), (SSAVE, 0), (RESULT, 0), (SAVE, 0), (SAVE, 2), (SAVE, 5), (SAVE, 1),
+    (SSAVE, 1), (SAVE, 3), (SAVE, 6), (SAVE, 4),
+)
+RELAY, PIPE_FIRST, PLANE_ONLY, PLANE_FIRST = range(4)
+WAYS = (RELAY, RELAY, RELAY, PLANE_FIRST, RELAY, PIPE_FIRST, PIPE_FIRST)
+DIRECT = (True, True, False, False, False, False, True)
+
+
+def grad_parts(state, model):
+    wide = 4 * state + model
+    return ((1, 4 * state, wide), (1, 2 * state, 4 * state), (1, 0, 2 * state), (0, 4 * state, wide), (0, 2 * state, 4 * state), (0, 0, state), (0, state, 2 * state))
+
+
+def weight_parts(state, model):
+    wide = 4 * state + model
+    return ((0, 0, state), (0, state, 2 * state), (0, 2 * state, 4 * state), (0, 4 * state, wide), (1, 0, 2 * state), (1, 2 * state, 4 * state), (1, 4 * state, wide))
+
+
 MESH = pl.DeviceIdType.MESH
 F32 = jnp.float32
 BF16 = jnp.bfloat16
 NN = (((1,), (0,)), ((), ()))
 NT = (((1,), (1,)), ((), ()))
 TN = (((0,), (0,)), ((), ()))
+FETCHES = ("lre", "lim", "lst", "b", "x", "c", "glu", "gain", "skip", "bias", "cot")
 
 
 def cmul(u, v):
@@ -62,110 +94,204 @@
     w_ref = refs["w"]
     sems = (refs["w_send"], refs["w_recv"])
     along, onward, across = {}, {}, {}
-
-    def part(piece):
-        layer, low, high = pieces[piece]
-        return w_ref.at[layer], pl.ds(low, high - low)
+    (to_x, by_x), (to_y, by_y) = neighbours(me, at_pipe)
+
+    def cols_of(piece, half=None):
+        _, low, high = pieces[piece]
+        middle = low + (high - low) // 256 * 128
+        return pl.ds(*((low, high - low), (low, middle - low), (middle, high - middle))[0 if half is None else half + 1])
+
+    def block(piece, z, member, half=None):
+        return w_ref.at[pieces[piece][0], z, core, member, :, cols_of(piece, half)]
 
     def send(piece):
-        ref, cols = part(piece)
-        along[piece] = []
-        for k in range(1, planes):
-            block = ref.at[plane, core, me, :, cols]
-            along[piece].append(remote(block, block, sems, (piece, k - 1), at_plane(k)))
+        own = block(piece, plane, me)
+        along[piece] = [remote(own, own, sems, (piece, k - 1), at_plane(k)) for k in range(1, planes)]
+
+    def place(k):
+        return lax.rem(plane - k + planes, planes)
 
     def relay(piece):
-        ref, cols = part(piece)
         onward[piece] = []
+        direct = DIRECT[piece]
         for k in range(1, planes):
             along[piece][k - 1].wait_recv()
-            block = ref.at[lax.rem(plane - k + planes, planes), core, me, :, cols]
-            for j in range(1, depth):
-                at = planes - 1 + (k - 1) * (depth - 1) + j - 1
-                onward[piece].append(remote(block, block, sems, (piece, at), at_pipe(j)))
+            own = block(piece, place(k), me)
+            for j, device in enumerate([at_pipe(j) for j in range(1, depth)] if direct else (to_x, to_y)):
+                onward[piece].append(remote(own, own, sems, (piece, planes - 1 + 4 * (k - 1) + j), device))
+
+    def forward(piece):
+        made = []
+        for k in range(1, planes):
+            for j, (member, device) in enumerate(((by_x, to_y), (by_y, to_x))):
+                onward[piece][2 * (k - 1) + j].wait_recv()
+                half = block(piece, place(k), member, j)
+                made.append(remote(half, half, sems, (piece, planes - 1 + 4 * (k - 1) + 2 + j), device))
+        onward[piece] = made
 
     def swap(piece):
-        ref, cols = part(piece)
         for copy in onward[piece]:
             copy.wait_recv()
-        block = ref.at[:, core, :, :, cols]
-        across[piece] = remote(block, block, sems, (piece, planes * depth - 1), at_core)
+        both = w_ref.at[pieces[piece][0], :, core, :, :, cols_of(piece)]
+        across[piece] = remote(both, both, sems, (piece, 5 * (planes - 1)), at_core)
 
     def ready(piece):
         across[piece].wait_recv()
 
-    return send, relay, swap, ready
-
-
-def gradient_sums(refs, orders, depth, planes, me, plane, core, at_pipe, at_plane, at_core, remote):
+    return send, relay, forward, swap, ready
+
+
+def neighbours(me, at_pipe):
+    x, y = lax.rem(me, 2), lax.div(me, 2)
+    by_x, by_y = 2 * y + 1 - x, 2 * (1 - y) + x
+    return (at_pipe(by_x - me + 4), by_x), (at_pipe(by_y - me + 4), by_y)
+
+
+def gradient_sums(refs, depth, planes, me, plane, core, at_pipe, at_plane, at_core, remote):
     sems = (refs["g_send"], refs["g_recv"])
     copies = {}
-    pipe_axis, plane_axis = (depth, me, at_pipe), (planes, plane, at_plane)
-
-    def axes(piece):
-        return (plane_axis, pipe_axis) if orders[piece] else (pipe_axis, plane_axis)
+    x, y = lax.rem(me, 2), lax.div(me, 2)
+    (to_x, by_x), (to_y, by_y) = neighbours(me, at_pipe)
+
+    def of(piece, *names):
+        return [refs[f"{name}{piece}"] for name in names]
+
+    def halves(piece):
+        width = refs[f"done{piece}"].shape[-1]
+        return pl.ds(0, width // 2), pl.ds(width // 2, width // 2)
+
+    def back_by_relay(piece):
+        return WAYS[piece] in (RELAY, PLANE_FIRST) and refs[f"done{piece}"].shape[-1] % 256 == 0
 
     def start(piece, matrix):
-        part, other = refs[f"part{piece}"], refs[f"other{piece}"]
+        part, other = of(piece, "part", "other")
         part[...] = matrix.astype(BF16).reshape(part.shape)
         copies[piece, 0] = remote(part.at[:, 1 - core], other, sems, (piece, 0), at_core)
 
     def first(piece):
         copies[piece, 0].wait_recv()
-        part, other, pair, quad = (refs[f"{name}{piece}"] for name in ("part", "other", "pair", "quad"))
+        part, other, pair, quad = of(piece, "part", "other", "pair", "quad")
 
         def add(i, carry):
             z, j = lax.div(i, depth), lax.rem(i, depth)
-            total = (part[z, core, j].astype(F32) + other[z, j].astype(F32)).astype(BF16)
-            if orders[piece]:
+            total = part[z, core, j] + other[z, j]
+            if WAYS[piece] in (PLANE_ONLY, PLANE_FIRST):
                 pair[z, j] = total
             else:
                 pair[j, z] = total
             return carry
         lax.fori_loop(0, planes * depth, add, 0, unroll=4)
-        count, here, there = axes(piece)[0]
-        copies[piece, 1] = [
-            remote(pair.at[lax.rem(here + k, count)], quad.at[k - 1], sems, (piece, k), there(k)) for k in range(1, count)
-        ]
-
-    def second(piece):
-        pair, quad, line, came = (refs[f"{name}{piece}"] for name in ("pair", "quad", "line", "came"))
+        if WAYS[piece] == RELAY:
+            low, high = halves(piece)
+            made = []
+            for i in range(2):
+                made.append(remote(pair.at[2 * i + 1 - x, :, :, low], quad.at[0, i], sems, (piece, 1 + i), to_x))
+                made.append(remote(pair.at[2 * (1 - y) + i, :, :, high], quad.at[1, i], sems, (piece, 3 + i), to_y))
+        else:
+            by_plane = WAYS[piece] in (PLANE_ONLY, PLANE_FIRST)
+            count, here, there = (planes, plane, at_plane) if by_plane else (depth, me, at_pipe)
+            made = [
+                remote(pair.at[lax.rem(here + k, count)], quad.at[k - 1], sems, (piece, k), there(k))
+                for k in range(1, count)
+            ]
+        copies[piece, 1] = made
+
+    def middle(piece):
+        pair, quad, pass_on, last = of(piece, "pair", "quad", "pass", "last")
         for copy in copies[piece, 1]:
             copy.wait_recv()
-        (count, here, _), (wide, there, go) = axes(piece)
-
-        def add(i, carry):
-            total = pair[here, i].astype(F32)
-            for k in range(1, count):
-                total = total + quad[k - 1, i].astype(F32)
-            line[i] = total.astype(BF16)
+        low, high = halves(piece)
+
+        def add(z, carry):
+            pass_on[0, z] = pair[by_y, z, :, low] + quad[0, 1 - y, z]
+            pass_on[1, z] = pair[by_x, z, :, high] + quad[1, 1 - x, z]
             return carry
-        lax.fori_loop(0, wide, add, 0, unroll=2)
+        lax.fori_loop(0, planes, add, 0, unroll=2)
         copies[piece, 2] = [
-            remote(line.at[lax.rem(there + k, wide)], came.at[k - 1], sems, (piece, count - 1 + k), go(k))
-            for k in range(1, wide)
+            remote(pass_on.at[0], last.at[0], sems, (piece, 5), to_y),
+            remote(pass_on.at[1], last.at[1], sems, (piece, 6), to_x),
         ]
 
+    def second(piece):
+        way = WAYS[piece]
+        pair, quad, line, came = of(piece, "pair", "quad", "line", "came")
+        for copy in copies[piece, 2 if way == RELAY else 1]:
+            copy.wait_recv()
+        if way == RELAY:
+            low, high = halves(piece)
+            last = refs[f"last{piece}"]
+
+            def add(z, carry):
+                for half, (cols, own) in enumerate(((low, y), (high, x))):
+                    total = pair[me, z, :, cols].astype(F32) + quad[half, own, z].astype(F32) + last[half, z].astype(F32)
+                    line[z, :, cols] = total.astype(BF16)
+                return carry
+        else:
+            here, count = (plane, planes) if way in (PLANE_ONLY, PLANE_FIRST) else (me, depth)
+
+            def add(i, carry):
+                total = pair[here, i].astype(F32)
+                for k in range(1, count):
+                    total = total + quad[k - 1, i].astype(F32)
+                if way == PLANE_ONLY:
+                    came[me, i] = total.astype(BF16)
+                else:
+                    line[i] = total.astype(BF16)
+                return carry
+        lax.fori_loop(0, depth if way in (PLANE_ONLY, PLANE_FIRST) else planes, add, 0, unroll=2)
+        if way == PLANE_ONLY:
+            made = [remote(came.at[me], came.at[me], sems, (piece, 6 + k), at_pipe(k)) for k in range(1, depth)]
+        elif way == PLANE_FIRST:
+            made = [
+                remote(line.at[lax.rem(me + k, depth)], came.at[k - 1], sems, (piece, 6 + k), at_pipe(k))
+                for k in range(1, depth)
+            ]
+        else:
+            made = [
+                remote(line.at[lax.rem(plane + k, planes)], came.at[k - 1], sems, (piece, 6 + k), at_plane(k))
+                for k in range(1, planes)
+            ]
+        copies[piece, 3] = made
+
     def third(piece):
-        line, came, done = (refs[f"{name}{piece}"] for name in ("line", "came", "done"))
-        for copy in copies[piece, 2]:
+        line, came, done = of(piece, "line", "came", "done")
+        for copy in copies[piece, 3]:
             copy.wait_recv()
-        wide, there, _ = axes(piece)[1]
-        total = line[there].astype(F32)
-        for k in range(1, wide):
+        by_plane = WAYS[piece] == PLANE_FIRST
+        total = line[me if by_plane else plane].astype(F32)
+        for k in range(1, depth if by_plane else planes):
             total = total + came[k - 1].astype(F32)
         done[me] = total.astype(BF16)
-        copies[piece, 3] = [
-            remote(done.at[me], done.at[me], sems, (piece, depth + planes + k - 2), at_pipe(k)) for k in range(1, depth)
+        devices = (to_x, to_y) if back_by_relay(piece) else [at_pipe(k) for k in range(1, depth)]
+        copies[piece, 4] = [
+            remote(done.at[me], done.at[me], sems, (piece, 6 + planes + i), device) for i, device in enumerate(devices)
         ]
 
+    def fourth(piece):
+        done = refs[f"done{piece}"]
+        low, high = halves(piece)
+        made = []
+        for i, (member, cols, device) in enumerate(((by_x, low, to_y), (by_y, high, to_x))):
+            copies[piece, 4][i].wait_recv()
+            half = done.at[member, :, cols]
+            made.append(remote(half, half, sems, (piece, 8 + planes + i), device))
+        copies[piece, 4] = made
+
     def finish(piece):
-        for copy in copies[piece, 3]:
-            copy.wait_recv()
-        done = refs[f"done{piece}"][...]
-        return done.reshape(done.shape[0] * done.shape[1], done.shape[2]).astype(F32)
-
-    return start, first, second, third, finish
+        if WAYS[piece] == PLANE_ONLY:
+            came = refs[f"came{piece}"]
+            for copy in copies[piece, 3]:
+                copy.wait_recv()
+            done = came[0].astype(F32)
+            for j in range(1, depth):
+                done = done + came[j].astype(F32)
+        else:
+            for copy in copies[piece, 4]:
+                copy.wait_recv()
+            done = refs[f"done{piece}"][...].astype(F32)
+        return done.reshape(done.shape[0] * done.shape[1], done.shape[2])
+
+    return start, first, middle, second, third, fourth, finish
 
 
 def small_sums(refs, depth, planes, me, plane, core, at_pipe, at_plane, at_core, remote):
@@ -208,8 +334,7 @@
 
 def main_kernel(depth, planes, names, *refs):
     r_ = dict(zip(names, refs))
-    x_ref, cot_ref, len_ref, gain_ref = r_["x"], r_["cot"], r_["len"], r_["gain"]
-    lre_ref, lim_ref, lst_ref, skip_ref, bias_ref = r_["lre"], r_["lim"], r_["lst"], r_["skip"], r_["bias"]
+    x_ref, len_ref = r_["x"], r_["len"]
     small_ref = r_["small"]
     h_ref, go_ref, xhat_ref, rstd_ref, normed_ref = r_["h"], r_["go"], r_["xhat"], r_["rstd"], r_["normed"]
     p_ref, z_ref, zb_ref, dg_ref, gated_ref, sig_ref = r_["p"], r_["z"], r_["zb"], r_["dg"], r_["gated"], r_["sig"]
@@ -217,8 +342,7 @@
     ends_ref, got_ref, send_sems, recv_sems = r_["ends"], r_["got"], r_["send"], r_["recv"]
     w_ref = r_["w"]
     seqs, pos, model = x_ref.shape
-    state = lre_ref.shape[1]
-    layers = gain_ref.shape[0]
+    layers, state = r_["lre"].shape
     rows = seqs * pos
     steps = pos // CHUNKS
     me, dp = lax.axis_index("pipe"), lax.axis_index("dp")
@@ -266,7 +390,7 @@
             return body(pl.ds(pl.multiple_of(q * pos + i * TILE, TILE), TILE), masks[q], carry)
         return lax.fori_loop(0, pos // TILE, step, init, unroll=unroll)
 
-    def all_tiles(body, init=0, unroll=2):
+    def all_tiles(body, init=0, unroll=4):
         for q in range(seqs):
             init = tiles(body, q, init, unroll)
         return init
@@ -278,17 +402,24 @@
         return total
 
     fetches = {}
-    for at, name in enumerate(("b", "x", "c", "glu", "cot") if planes else ("x", "cot")):
+    for at, name in enumerate(FETCHES):
+        if name not in r_:
+            continue
         fetches[name] = pltpu.make_async_copy(r_[name], r_[name + "_here"], r_["fetch"].at[at])
         fetches[name].start()
     x_here, cot_here = r_["x_here"], r_["cot_here"]
+    gain_ref, skip_ref, bias_ref = r_["gain_here"], r_["skip_here"], r_["bias_here"]
+    lre_ref, lim_ref, lst_ref = r_["lre_here"], r_["lim_here"], r_["lst_here"]
+    for name in ("lre", "lim", "lst"):
+        fetches[name].wait()
     step_all, decay_all, coef_all = discretize(lre_ref[...], lim_ref[...], lst_ref[...])
     if planes:
         ways = (depth, planes, me, plane, core, at_pipe, at_plane, at_core, remote)
         wide = 4 * state + model
-        pieces = ((0, 0, 2 * state), (0, 2 * state, wide), (1, 0, 2 * state), (1, 2 * state, wide))
-        w_send, w_relay, w_swap, w_ready = weight_gather(r_, pieces, *ways)
-        g_start, g_first, g_second, g_third, g_finish = gradient_sums(r_, GRAD_ORDERS, *ways)
+        pieces = weight_parts(state, model)
+        w_send, w_relay, w_forward, w_swap, w_ready = weight_gather(r_, pieces, *ways)
+        g_start, g_first, g_middle, g_second, g_third, g_fourth, g_finish = gradient_sums(r_, *ways)
+        parts = grad_parts(state, model)
         s_start, s_pipe, s_plane, s_finish = small_sums(r_, *ways)
 
         def keep(layer, matrix, low):
@@ -299,22 +430,6 @@
         for layer in range(layers):
             keep(layer, r_["b_here"][layer], 0)
     pl.semaphore_wait(barrier, len(others))
-    if planes:
-        w_send(0)
-        fetches["c"].wait()
-        fetches["glu"].wait()
-        for layer in range(layers):
-            coef = (coef_all[0][layer:layer + 1], coef_all[1][layer:layer + 1])
-            turned = cmul(coef, (r_["c_here"][layer, :, 0:state], r_["c_here"][layer, :, state:2 * state]))
-            keep(layer, turned[0], 2 * state)
-            keep(layer, -turned[1], 3 * state)
-            keep(layer, r_["glu_here"][layer], 4 * state)
-        w_send(1)
-        w_send(2)
-        w_send(3)
-    fetches["x"].wait()
-    for q in range(seqs):
-        h_ref[0, seq_rows(q), :] = dot(spread, x_here[q], NN).astype(BF16)
 
     def matrix(layer, which):
         low, high = (0, 2 * state, 4 * state)[which], (2 * state, 4 * state, w_ref.shape[-1])[which]
@@ -336,7 +451,7 @@
                 moved = cmul(decay, carry[q])
                 made.append((moved[0] + add[0], moved[1] + add[1]))
             return tuple(made)
-        return lax.fori_loop(0, steps, step, ((zero, zero),) * seqs, unroll=4)
+        return lax.fori_loop(0, steps, step, ((zero, zero),) * seqs, unroll=32)
 
     def shifted(value, k, down):
         rolled = pltpu.roll(value, CHUNKS - k if down else k, axis=0)
@@ -421,55 +536,80 @@
     def back_powers(layer):
         return [conj(power) for power in powers_of[layer]]
 
-    for layer in range(layers):
-        down = layer % 2 == 1
-        decay = wide_decay(layer)
-        gain = gain_ref[layer:layer + 1, :]
-        skip = skip_ref[layer:layer + 1, :]
-        bias = bias_ref[layer:layer + 1, :]
-
-        def norm_tile(r, mask, carry):
+    pad = pos + CHUNKS
+    gather = (lax.rem(row, steps) * CHUNKS + lax.div(row, steps) == col).astype(F32).astype(BF16)
+    zero_row = jnp.zeros((8, model), F32)
+    puts, held = [], {}
+
+    def put(name, at=None, cols=None):
+        source, target = r_[name + "_here"], r_[name]
+        if cols is not None:
+            source, target = source.at[at, :, cols], target.at[at, :, cols]
+        elif at is not None:
+            source, target = source.at[at], target.at[at]
+        copy = pltpu.make_async_copy(source, target, r_["put"].at[len(puts)])
+        copy.start()
+        puts.append(copy)
+
+    def one(ref, layer):
+        return ref[layer:layer + 1, :]
+
+    def turn(layer, real, imag):
+        return cmul((coef_all[0][layer:layer + 1], coef_all[1][layer:layer + 1]), (real, imag))
+
+    def step_fold(layer):
+        if layer == 0:
+            fetches["c"].wait()
+            fetches["glu"].wait()
+        turned = turn(layer, r_["c_here"][layer, :, 0:state], r_["c_here"][layer, :, state:2 * state])
+        keep(layer, turned[0], 2 * state)
+        keep(layer, -turned[1], 3 * state)
+        keep(layer, r_["glu_here"][layer], 4 * state)
+
+    def step_x(_):
+        for name in ("x", "gain", "skip", "bias"):
+            fetches[name].wait()
+        for q in range(seqs):
+            h_ref[0, seq_rows(q), :] = dot(spread, x_here[q], NN).astype(BF16)
+
+    def step_cot(_):
+        fetches["cot"].wait()
+        for q in range(seqs):
+            go_ref[seq_rows(q), :] = dot(spread, cot_here[q], NN).astype(BF16)
+
+    def step_norm(layer):
+        gain = one(gain_ref, layer)
+
+        def tile(r, mask, carry):
             h = h_ref[layer, r, :].astype(F32)
             mean = jnp.mean(h, axis=1, keepdims=True)
             centred = h - mean
-            spread_ = jnp.mean(centred * centred, axis=1, keepdims=True)
-            rstd = lax.rsqrt(spread_ + EPSILON)
+            variance = jnp.mean(centred * centred, axis=1, keepdims=True)
+            rstd = lax.rsqrt(variance + EPSILON)
             xhat = centred * rstd
             xhat_ref[layer, r, :] = xhat
             rstd_ref[layer, r, :] = jnp.broadcast_to(rstd, (TILE, 128))
             normed_ref[layer, r, :] = (xhat * gain * mask).astype(BF16)
             return carry
-        all_tiles(norm_tile, unroll=4)
-
-        if layer == 0:
-            if planes:
-                w_relay(0)
-            fetches["cot"].wait()
-            for q in range(seqs):
-                go_ref[seq_rows(q), :] = dot(spread, cot_here[q], NN).astype(BF16)
-        if planes and layer == 0:
-            w_relay(1)
-            w_swap(0)
-            w_ready(0)
-        if planes and layer == 1:
-            w_ready(2)
+        all_tiles(tile, unroll=4)
+
+    def step_proj(layer):
         p_ref[layer] = dot(normed_ref[layer], matrix(layer, 0), NN)
-        ends = scan_ends(p_ref.at[layer], decay, down)
-        pending = start_exchange(layer, ends, powers_of[layer], down)
-        if planes and layer == 0:
-            w_relay(2)
-            w_relay(3)
-            w_swap(1)
-        if planes and layer == 1:
-            w_swap(3)
-        carries = finish_exchange(layer, pending, powers_of[layer], down)
-        pad = pos + CHUNKS
+
+    def step_ends(layer):
+        ends = scan_ends(p_ref.at[layer], wide_decay(layer), layer % 2 == 1)
+        held["pending", layer] = start_exchange(layer, ends, powers_of[layer], layer % 2 == 1)
+
+    def step_scan(layer):
+        down = layer % 2 == 1
+        decay = wide_decay(layer)
+        carries = finish_exchange(layer, held["pending", layer], powers_of[layer], down)
         for q in range(seqs):
             at = q * pad + (pos if down else 0)
             z_ref[layer, at:at + CHUNKS, 0:state] = carries[q][0]
             z_ref[layer, at:at + CHUNKS, state:2 * state] = carries[q][1]
 
-        def state_pair(i, carry):
+        def pair(i, carry):
             carry = list(carry)
             for q in range(seqs):
                 pieces = []
@@ -491,97 +631,75 @@
                     both = jnp.concatenate([pieces[0][part], pieces[1][part]], axis=0)
                     zb_ref[layer, r, part * state:(part + 1) * state] = both.astype(BF16)
             return tuple(carry)
-        lax.fori_loop(0, steps // 2, state_pair, tuple(carries), unroll=2)
-
-        if planes:
-            w_ready(2 * layer + 1)
+        lax.fori_loop(0, steps // 2, pair, tuple(carries), unroll=16)
+
+    def step_cdot(layer):
         tmp_ref[...] = dot(zb_ref[layer], matrix(layer, 1), NT)
 
-        def gelu_tile(r, mask, carry):
+    def step_gelu(layer):
+        skip = one(skip_ref, layer)
+
+        def tile(r, mask, carry):
             before = tmp_ref[r, :] + skip * normed_ref[layer, r, :].astype(F32)
             phi = 0.5 * (1.0 + lax.erf(before * 0.7071067811865476))
             dg_ref[layer, r, :] = phi + before * (0.3989422804014327 * jnp.exp(-0.5 * before * before))
             gated_ref[layer, r, :] = (before * phi).astype(BF16)
             return carry
-        all_tiles(gelu_tile)
-
+        all_tiles(tile)
+
+    def step_gdot(layer):
         tmp_ref[...] = dot(gated_ref[layer], matrix(layer, 2), NN)
 
-        def out_tile(r, mask, carry):
+    def step_out(layer):
+        bias = one(bias_ref, layer)
+
+        def tile(r, mask, carry):
             sig = 1.0 / (1.0 + jnp.exp(-(tmp_ref[r, :] + bias)))
             sig_ref[layer, r, :] = sig
             made = h_ref[layer, r, :].astype(F32) + mask * (gated_ref[layer, r, :].astype(F32) * sig)
             h_ref[layer + 1, r, :] = made.astype(BF16)
             return carry
-        if planes and layer == 0:
-            w_swap(2)
-        all_tiles(out_tile)
-
-    puts = []
-
-    def put(name, at=None):
-        source, target = r_[name + "_here"], r_[name]
-        if at is not None:
-            source, target = source.at[at], target.at[at]
-        copy = pltpu.make_async_copy(source, target, r_["put"].at[len(puts)])
-        copy.start()
-        puts.append(copy)
-
-    gather = (lax.rem(row, steps) * CHUNKS + lax.div(row, steps) == col).astype(F32).astype(BF16)
-    for q in range(seqs):
-        r_["out_here"][q] = dot(gather, h_ref[layers, seq_rows(q), :], NN).astype(BF16)
-    put("out")
-
-    for layer in reversed(range(layers)):
-        down = layer % 2 == 1
-        decay = wide_decay(layer)
-        gain = gain_ref[layer:layer + 1, :]
-        skip = skip_ref[layer:layer + 1, :]
-        zero_row = jnp.zeros((8, model), F32)
-
-        def gate_tile(r, mask, carry):
+        all_tiles(tile)
+
+    def step_result(_):
+        for q in range(seqs):
+            r_["out_here"][q] = dot(gather, h_ref[layers, seq_rows(q), :], NN).astype(BF16)
+        put("out")
+
+    def step_gate(layer):
+        def tile(r, mask, carry):
             sig = sig_ref[layer, r, :]
             branch = mask * go_ref[r, :].astype(F32) * sig
             grad = (branch * gated_ref[layer, r, :].astype(F32) * (1.0 - sig)).astype(BF16)
             gg_ref[r, :] = grad
             acc_ref[r, :] = branch
             return carry + fold(grad.astype(F32))
-        bias_sum = all_tiles(gate_tile, zero_row)
-        if planes and layer == 0:
-            g_start(G0, dot(gated_ref[layer], gg_ref[...], TN))
+        held["bias", layer] = all_tiles(tile, zero_row)
+
+    def step_gback(layer):
         tmp_ref[...] = dot(gg_ref[...], matrix(layer, 2), NT)
 
-        def before_tile(r, mask, carry):
+    def step_before(layer):
+        def tile(r, mask, carry):
             gated_grad = (acc_ref[r, :] + tmp_ref[r, :]).astype(BF16).astype(F32)
             grad = (gated_grad * dg_ref[layer, r, :]).astype(BF16)
             gb_ref[r, :] = grad
             return carry + fold(grad.astype(F32) * normed_ref[layer, r, :].astype(F32))
-        skip_sum = all_tiles(before_tile, zero_row)
-
-        if planes and layer == 0:
-            g_first(G0)
+        held["skip", layer] = all_tiles(tile, zero_row)
+
+    def step_src(layer):
         src_ref[...] = dot(gb_ref[...], matrix(layer, 1), NN)
-        back = conj(decay)
-        ends = scan_ends(src_ref, back, not down)
-        pending = start_exchange(layers + layer, ends, back_powers(layer), not down)
-        if planes and layer == 0:
-            g_first(B1)
-        c_part = dot(gb_ref[...], zb_ref[layer], TN)
-        if not planes:
-            r_["gpart"][layer, :, 4 * state:] = dot(gated_ref[layer], gg_ref[...], TN)
-            r_["gpart"][layer, :, 2 * state:4 * state] = c_part
-        elif layer == 1:
-            g_start(C1, c_part)
-            g_start(G1, dot(gated_ref[layer], gg_ref[...], TN))
-            g_first(C1)
-        else:
-            g_start(C0, c_part)
-            g_second(C1)
-            s_pipe(1)
-            g_first(C0)
-        carries = finish_exchange(layers + layer, pending, back_powers(layer), not down)
-
-        def adjoint_pair(i, loop):
+
+    def step_bends(layer):
+        ends = scan_ends(src_ref, conj(wide_decay(layer)), layer % 2 == 0)
+        held["back", layer] = start_exchange(layers + layer, ends, back_powers(layer), layer % 2 == 0)
+
+    def step_bscan(layer):
+        down = layer % 2 == 1
+        back = conj(wide_decay(layer))
+        carries = finish_exchange(layers + layer, held["back", layer], back_powers(layer), not down)
+
+        def pair(i, loop):
             carry, sums = list(loop[0]), list(loop[1])
             for q in range(seqs):
                 pieces = []
@@ -608,22 +726,33 @@
                     both = jnp.concatenate([pieces[0][part], pieces[1][part]], axis=0)
                     gp_ref[r, part * state:(part + 1) * state] = both.astype(BF16)
             return tuple(carry), tuple(sums)
-        _, sums = lax.fori_loop(0, steps // 2, adjoint_pair, (tuple(carries), (zero,) * 4), unroll=1)
-
-        b_part = dot(normed_ref[layer], gp_ref[...], TN)
+        held["sums", layer] = lax.fori_loop(0, steps // 2, pair, (tuple(carries), (zero,) * 4), unroll=16)[1]
+
+    def send_part(layer, low, made):
+        high = low + made.shape[1]
         if not planes:
-            r_["gpart"][layer, :, 0:2 * state] = b_part
-        elif layer == 1:
-            g_start(B1, b_part)
-            g_first(G1)
-        else:
-            g_start(B0, b_part)
+            r_["gpart"][layer, :, low:high] = made
+            return
+        for piece, (of_layer, first, last) in enumerate(parts):
+            if of_layer == layer and low <= first and last <= high:
+                g_start(piece, made[:, first - low:last - low])
+
+    def step_cgrad(layer):
+        send_part(layer, 2 * state, dot(gb_ref[...], zb_ref[layer], TN))
+
+    def step_ggrad(layer):
+        send_part(layer, 4 * state, dot(gated_ref[layer], gg_ref[...], TN))
+
+    def step_bgrad(layer):
+        send_part(layer, 0, dot(normed_ref[layer], gp_ref[...], TN))
+
+    def step_xdot(layer):
         tmp_ref[...] = dot(gp_ref[...], matrix(layer, 0), NT)
-        if planes and layer == 0:
-            g_first(B0)
-            g_second(G1)
-
-        def input_tile(r, mask, carry):
+
+    def step_bnorm(layer):
+        gain, skip = one(gain_ref, layer), one(skip_ref, layer)
+
+        def tile(r, mask, carry):
             grad = (tmp_ref[r, :] + skip * gb_ref[r, :].astype(F32)) * mask
             xhat = xhat_ref[layer, r, :]
             rstd = jnp.concatenate([rstd_ref[layer, r, :]] * (model // 128), axis=1)
@@ -633,69 +762,63 @@
             made = go_ref[r, :].astype(F32) + rstd * (scaled - first - xhat * second)
             go_ref[r, :] = made.astype(BF16)
             return carry + fold(grad * xhat)
-        gain_sum = all_tiles(input_tile, zero_row, unroll=4)
-
-        for at, value in enumerate((gain_sum, skip_sum, bias_sum)):
+        gain_sum = all_tiles(tile, zero_row, unroll=4)
+        for at, value in enumerate((gain_sum, held["skip", layer], held["bias", layer])):
             small_ref[layer, at:at + 1, :] = jnp.sum(value, axis=0, keepdims=True)
-        for at, value in enumerate(sums):
+        for at, value in enumerate(held["sums", layer]):
             small_ref[layer, 3 + at:4 + at, 0:state] = jnp.sum(value, axis=0, keepdims=True)
-        if planes:
-            s_start(layer)
-
-    for q in range(seqs):
-        r_["xg_here"][q] = dot(gather, go_ref[seq_rows(q), :], NN).astype(BF16)
-    put("xg")
-    if planes:
-        def store_small(layer):
-            total = s_finish(layer)
-            for at, name in enumerate(("gain_grad", "skip_grad", "bias_grad")):
-                r_[name][layer:layer + 1, :] = total[at:at + 1, :]
-            one = slice(layer, layer + 1)
-            coef = (coef_all[0][one], coef_all[1][one])
-            sums = [total[at:at + 1, 0:state] for at in range(3, 7)]
-            scale = coef[0] * coef[0] + coef[1] * coef[1]
-            coef_grad = cmul((sums[2], sums[3]), (coef[0] / scale, coef[1] / scale))
-            made = discretize_grads(lre_ref[one], lim_ref[one], lst_ref[one], (sums[0], sums[1]), coef_grad)
-            for name, value in zip(("lre_grad", "lim_grad", "lst_grad"), made):
-                r_[name][one, :] = value
-
-        def store_b(layer, piece):
-            r_["b_grad_here"][layer] = g_finish(piece)
-            put("b_grad", layer)
-
-        def store_c(layer, piece):
-            coef = (coef_all[0][layer:layer + 1], coef_all[1][layer:layer + 1])
-            done = g_finish(piece)
-            turned = cmul(coef, (done[:, 0:state], done[:, state:2 * state]))
+
+    def step_xg(_):
+        for q in range(seqs):
+            r_["xg_here"][q] = dot(gather, go_ref[seq_rows(q), :], NN).astype(BF16)
+        put("xg")
+
+    def step_ssave(layer):
+        total = s_finish(layer)
+        for at, name in enumerate(("gain_grad", "skip_grad", "bias_grad")):
+            r_[name + "_here"][layer:layer + 1, :] = total[at:at + 1, :]
+        coef = (coef_all[0][layer:layer + 1], coef_all[1][layer:layer + 1])
+        sums = [total[at:at + 1, 0:state] for at in range(3, 7)]
+        scale = coef[0] * coef[0] + coef[1] * coef[1]
+        coef_grad = cmul((sums[2], sums[3]), (coef[0] / scale, coef[1] / scale))
+        made = discretize_grads(
+            one(lre_ref, layer), one(lim_ref, layer), one(lst_ref, layer), (sums[0], sums[1]), coef_grad)
+        for name, value in zip(("lre_grad", "lim_grad", "lst_grad"), made):
+            r_[name + "_here"][layer:layer + 1, :] = value
+
+    def step_save(piece):
+        layer, low, high = parts[piece]
+        done = g_finish(piece)
+        if low >= 4 * state:
+            r_["glu_grad_here"][layer] = done
+            put("glu_grad", layer)
+        elif low >= 2 * state:
+            turned = turn(layer, done[:, 0:state], done[:, state:2 * state])
             r_["c_grad_here"][layer, :, 0:state] = turned[0]
             r_["c_grad_here"][layer, :, state:2 * state] = -turned[1]
             put("c_grad", layer)
-
-        def store_glu(layer, piece):
-            r_["glu_grad_here"][layer] = g_finish(piece)
-            put("glu_grad", layer)
-
-        s_pipe(0)
-        s_plane(1)
-        g_second(B1)
-        g_third(C1)
-        g_second(G0)
-        g_second(C0)
-        g_third(G1)
-        g_second(B0)
-        s_plane(0)
-        g_third(B1)
-        g_third(G0)
-        store_small(1)
-        store_c(1, C1)
-        store_glu(1, G1)
-        g_third(C0)
-        store_b(1, B1)
-        g_third(B0)
-        store_small(0)
-        store_glu(0, G0)
-        store_c(0, C0)
-        store_b(0, B0)
+        else:
+            r_["b_grad_here"][layer, :, low:high] = done
+            put("b_grad", layer, pl.ds(low, high - low))
+
+    do = {
+        X: step_x, COT: step_cot, NORM: step_norm, PROJ: step_proj, ENDS: step_ends, SCAN: step_scan, CDOT: step_cdot,
+        GELU: step_gelu, GDOT: step_gdot, OUT: step_out, RESULT: step_result, GATE: step_gate, GBACK: step_gback,
+        BEFORE: step_before, SRC: step_src, BENDS: step_bends, BSCAN: step_bscan, CGRAD: step_cgrad, GGRAD: step_ggrad,
+        BGRAD: step_bgrad, XDOT: step_xdot, BNORM: step_bnorm, XG: step_xg,
+    }
+    if planes:
+        do.update({
+            FOLD: step_fold, WSEND: w_send, WRELAY: w_relay, WFORWARD: w_forward, WSWAP: w_swap, WREADY: w_ready,
+            FIRST: g_first, MIDDLE: g_middle, SECOND: g_second, THIRD: g_third, FOURTH: g_fourth, SAVE: step_save,
+            SSTART: s_start, SPIPE: s_pipe, SPLANE: s_plane, SSAVE: step_ssave,
+        })
+    for name, at in ORDER:
+        if name in do:
+            do[name](at)
+    if planes:
+        for name in ("gain_grad", "skip_grad", "bias_grad", "lre_grad", "lim_grad", "lst_grad"):
+            put(name)
     for copy in puts:
         copy.wait()
     for copy in unsent:
@@ -762,8 +885,8 @@
         acc=pltpu.VMEM((rows, model), F32),
         ends=pltpu.VMEM((2 * layers, message, 128), F32),
         got=pltpu.VMEM((2 * layers, depth - 1, message, 128), F32),
-        fetch=pltpu.SemaphoreType.DMA((5,)),
-        put=pltpu.SemaphoreType.DMA((8,)),
+        fetch=pltpu.SemaphoreType.DMA((len(FETCHES),)),
+        put=pltpu.SemaphoreType.DMA((8 + len(WAYS),)),
         send=pltpu.SemaphoreType.DMA((2 * layers, depth - 1)),
         recv=pltpu.SemaphoreType.DMA((2 * layers, depth - 1)),
     )
@@ -783,29 +906,32 @@
             s_line=pltpu.VMEM((layers, planes, 8, model), F32),
             w=pltpu.VMEM((layers, planes, 2, depth, part, wide), BF16),
         )
-        for piece, first_plane in enumerate(GRAD_ORDERS):
-            width = model if piece in (G0, G1) else 2 * state
-            count, other = (planes, depth) if first_plane else (depth, planes)
-            scratch.update({
-                f"part{piece}": pltpu.VMEM((planes, 2, depth, part, width), BF16),
-                f"other{piece}": pltpu.VMEM((planes, depth, part, width), BF16),
-                f"pair{piece}": pltpu.VMEM((count, other, part, width), BF16),
-                f"quad{piece}": pltpu.VMEM((count - 1, other, part, width), BF16),
-                f"line{piece}": pltpu.VMEM((other, part, width), BF16),
-                f"came{piece}": pltpu.VMEM((other - 1, part, width), BF16),
-                f"done{piece}": pltpu.VMEM((depth, part, width), BF16),
-            })
+        spans = [high - low for _, low, high in grad_parts(state, model)]
+        for piece, way in enumerate(WAYS):
+            width = spans[piece]
+            count, other = (planes, depth) if way in (PLANE_ONLY, PLANE_FIRST) else (depth, planes)
+            shapes = dict(
+                part=(planes, 2, depth, part, width), other=(planes, depth, part, width),
+                pair=(count, other, part, width), quad=(count - 1, other, part, width),
+                line=(other, part, width), came=(other - 1, part, width), done=(depth, part, width),
+            )
+            if way == RELAY:
+                shapes.update(quad=(2, 2, planes, part, width // 2))
+                shapes.update({"pass": (2, planes, part, width // 2), "last": (2, planes, part, width // 2)})
+            if way == PLANE_ONLY:
+                shapes.update(came=(depth, depth, part, width))
+            scratch.update({f"{name}{piece}": pltpu.VMEM(shape, BF16) for name, shape in shapes.items()})
         for name, shape in dict(
-            w=(4, planes * depth), g=(6, 2 * depth + planes - 2), s=(layers, depth + planes - 1)
+            w=(len(DIRECT), 5 * planes - 4), g=(len(WAYS), 10 + planes), s=(layers, depth + planes - 1)
         ).items():
             scratch[name + "_send"] = pltpu.SemaphoreType.DMA(shape)
             scratch[name + "_recv"] = pltpu.SemaphoreType.DMA(shape)
     else:
         outs.update(gpart=((layers, model, wide), F32), small=((layers, 8, model), F32))
-    fetched = ("x", "cot", "b", "c", "glu") if planes else ("x", "cot")
+    fetched = tuple(name for name in FETCHES if name in ins)
     for name in fetched:
         scratch[name + "_here"] = pltpu.VMEM(ins[name].shape, ins[name].dtype)
-    stored = ("out", "xg", "b_grad", "c_grad", "glu_grad") if planes else ("out", "xg")
+    stored = tuple(name for name in outs if name not in ("gpart", "small"))
     for name in stored:
         scratch[name + "_here"] = pltpu.VMEM(*outs[name])
     names = tuple(ins) + tuple(outs) + tuple(scratch)
@@ -828,7 +954,7 @@
     depth, owners = lax.axis_size("pipe"), lax.axis_size("dp")
     state = lambda_re.shape[1]
     rest = (lambda_re, lambda_im, log_step, skip_weight, glu_bias)
-    if b_weight.shape[1] % (16 * depth) == 0 and owners % 2 == 0:
+    if depth == 4 and b_weight.shape[1] % (16 * depth) == 0 and owners % 2 == 0:
         return copied(run_main(owners // 2, x_in, lengths, cotangent, norm_gain, *rest, (b_weight, c_weight, glu_weight)))
     _, _, coef = discretize(lambda_re, lambda_im, log_step)
     c_real, c_imag = c_weight[:, :, :state], c_weight[:, :, state:]

time: 78.7 us -> 72.5 us (0.921)
  Pallas kernels: 77.9 us -> 71.5 us
    pallas_call x1, Pallas kernels: 75.3 us -> 69 us  [run_main(): pl.pallas_call(functools.partial(main_kernel, depth, planes, names), out_...]
where the time goes in v4:
time: 72.5 us; the launch traced here: 72.4 us
  Pallas kernels  71.5 us (99%)
  between operations  0.82 us (1%)
    pallas_call x1, Pallas kernels, run_main(): pl.pallas_call(functools.partial(main_kernel, depth, planes, names), out_...  69 us
    pallas_call x1, Pallas kernels, copied(): pl.pallas_call(copy_kernel, out_shape=tuple((jax.ShapeDtypeStruct(r.shape...  2.57 us

profile of v4, /device:TPU:0, one launch (start us, length us, event | category | flops | bytes accessed | tf_op | source)
XLA Modules:
  0.0 72.4 jit_solution(5486780053963645959)
XLA Ops:
  0.6 69.0 %shard_map.203 = (bf16[2,256,512]{2,1,0:T(8,128)(2,1)}, bf16[2,256,512]{2,1,0:T(8,128)(2,1)}, f32[2,512]{1,0:T(2,128)}, f32[2,384]{1,0:T(2,128)}, f32[2,384]{1,0...) custom-call(bf16[2,256,512]{2,1,0:T(8,128)(2,1)} %refs_0_.1, ...), custom_call_target="tpu_custom_call" | custom-call | tf_op jit(solution)/shard_map/pallas_call | solution.py:938
  69.6 2.6 %shard_map.204 = (bf16[2,256,512]{2,1,0:T(8,128)(2,1)}, bf16[2,256,512]{2,1,0:T(8,128)(2,1)}, f32[2,512]{1,0:T(2,128)}, f32[2,384]{1,0:T(2,128)}, f32[2,384]{1,0...) custom-call(bf16[2,256,512]{2,1,0:T(8,128)(2,1)} %get-tuple-element., ...), custom_call_target="tpu_custom_call" | custom-call | tf_op jit(solution)/shard_map/pallas_call | solution.py:844

commit v5 on v4

--- a/solution.py
+++ b/solution.py
@@ -13,20 +13,20 @@
 X, COT, NORM, PROJ, ENDS, SCAN, CDOT, GELU, GDOT, OUT, RESULT, GATE, GBACK, BEFORE, SRC, BENDS, BSCAN, CGRAD, GGRAD, BGRAD, XDOT, BNORM, XG = range(23)
 FOLD, WSEND, WRELAY, WFORWARD, WSWAP, WREADY, FIRST, MIDDLE, SECOND, THIRD, FOURTH, SAVE, SSTART, SPIPE, SPLANE, SSAVE = range(23, 39)
 ORDER = (
-    (WSEND, 1), (X, 0), (WSEND, 0), (FOLD, 0), (FOLD, 1), (WSEND, 4), (WSEND, 3), (WRELAY, 1), (WRELAY, 0),
-    (WSEND, 2), (WRELAY, 4), (WSWAP, 1), (WSEND, 6), (WRELAY, 3), (WSWAP, 0), (WSEND, 5), (COT, 0), (WRELAY, 2),
-    (WFORWARD, 4), (WFORWARD, 3), (WREADY, 1), (WREADY, 0), (NORM, 0), (PROJ, 0), (ENDS, 0), (WFORWARD, 2),
-    (WSWAP, 4), (WRELAY, 5), (WSWAP, 3), (WREADY, 3), (WSWAP, 2), (WRELAY, 6), (WREADY, 4), (SCAN, 0), (WREADY, 2),
-    (CDOT, 0), (GELU, 0), (WFORWARD, 5), (GDOT, 0), (OUT, 0), (NORM, 1), (PROJ, 1), (ENDS, 1), (WSWAP, 5), (WSWAP, 6),
-    (WREADY, 6), (WREADY, 5), (SCAN, 1), (CDOT, 1), (GELU, 1), (GDOT, 1), (OUT, 1), (GATE, 1), (GBACK, 1),
-    (BEFORE, 1), (SRC, 1), (BENDS, 1), (CGRAD, 1), (GGRAD, 1), (FIRST, 0), (FIRST, 1), (BSCAN, 1), (XDOT, 1),
-    (BGRAD, 1), (BNORM, 1), (GATE, 0), (GGRAD, 0), (GBACK, 0), (MIDDLE, 0), (BEFORE, 0), (FIRST, 2), (CGRAD, 0),
-    (FIRST, 3), (SRC, 0), (BENDS, 0), (FIRST, 4), (SECOND, 0), (MIDDLE, 1), (MIDDLE, 2), (BSCAN, 0), (BGRAD, 0),
-    (SSTART, 1), (MIDDLE, 4), (SECOND, 1), (FIRST, 5), (FIRST, 6), (XDOT, 0), (SECOND, 2), (SECOND, 3), (BNORM, 0),
-    (SSTART, 0), (SECOND, 4), (SPIPE, 0), (THIRD, 1), (SPIPE, 1), (SECOND, 5), (THIRD, 0), (SECOND, 6), (THIRD, 2),
-    (THIRD, 3), (SPLANE, 0), (FOURTH, 1), (XG, 0), (THIRD, 4), (SPLANE, 1), (FOURTH, 0), (THIRD, 5), (FOURTH, 2),
-    (FOURTH, 3), (THIRD, 6), (FOURTH, 4), (SSAVE, 0), (RESULT, 0), (SAVE, 0), (SAVE, 2), (SAVE, 5), (SAVE, 1),
-    (SSAVE, 1), (SAVE, 3), (SAVE, 6), (SAVE, 4),
+    (WSEND, 0), (WSEND, 1), (X, 0), (WSEND, 4), (FOLD, 0), (NORM, 0), (WSEND, 2), (FOLD, 1), (WSEND, 3), (WSEND, 5),
+    (WRELAY, 0), (WRELAY, 1), (WRELAY, 4), (WSWAP, 0), (WRELAY, 2), (WSWAP, 1), (WRELAY, 3), (WREADY, 0), (WREADY, 1),
+    (PROJ, 0), (WFORWARD, 4), (ENDS, 0), (WSEND, 6), (WFORWARD, 2), (COT, 0), (WFORWARD, 3), (WRELAY, 5), (WSWAP, 4),
+    (WSWAP, 2), (WRELAY, 6), (WREADY, 4), (WSWAP, 3), (SCAN, 0), (WREADY, 2), (CDOT, 0), (GELU, 0), (WREADY, 3),
+    (WFORWARD, 5), (GDOT, 0), (OUT, 0), (NORM, 1), (PROJ, 1), (ENDS, 1), (WSWAP, 6), (WSWAP, 5), (WREADY, 5),
+    (WREADY, 6), (SCAN, 1), (CDOT, 1), (GELU, 1), (GDOT, 1), (OUT, 1), (GATE, 1), (GBACK, 1), (BEFORE, 1), (SRC, 1),
+    (BENDS, 1), (GGRAD, 1), (CGRAD, 1), (FIRST, 1), (FIRST, 0), (BSCAN, 1), (BGRAD, 1), (XDOT, 1), (BNORM, 1),
+    (GATE, 0), (GGRAD, 0), (FIRST, 2), (GBACK, 0), (BEFORE, 0), (CGRAD, 0), (FIRST, 3), (MIDDLE, 1), (SRC, 0),
+    (BENDS, 0), (FIRST, 4), (MIDDLE, 0), (MIDDLE, 2), (SECOND, 1), (BSCAN, 0), (BGRAD, 0), (MIDDLE, 4), (XDOT, 0),
+    (SSTART, 1), (SECOND, 0), (BNORM, 0), (FIRST, 6), (SSTART, 0), (RESULT, 0), (SECOND, 2), (FIRST, 5), (SECOND, 3),
+    (SPIPE, 0), (SECOND, 4), (SECOND, 6), (SPIPE, 1), (THIRD, 1), (SECOND, 5), (XG, 0), (THIRD, 0), (THIRD, 2),
+    (THIRD, 3), (SPLANE, 0), (THIRD, 4), (THIRD, 6), (FOURTH, 1), (SPLANE, 1), (FOURTH, 2), (FOURTH, 0), (FOURTH, 3),
+    (THIRD, 5), (FOURTH, 4), (SSAVE, 0), (SAVE, 1), (SAVE, 6), (SAVE, 3), (SAVE, 2), (SAVE, 0), (SSAVE, 1), (SAVE, 4),
+    (SAVE, 5),
 )
 RELAY, PIPE_FIRST, PLANE_ONLY, PLANE_FIRST = range(4)
 WAYS = (RELAY, RELAY, RELAY, PLANE_FIRST, RELAY, PIPE_FIRST, PIPE_FIRST)

time: 72.5 us -> 72.1 us (level)
  no operation moved by 1% of the time
where the time goes in v5:
time: 72.1 us; the launch traced here: 71.9 us
  Pallas kernels  71.1 us (99%)
  between operations  0.82 us (1%)
    pallas_call x1, Pallas kernels, run_main(): pl.pallas_call(functools.partial(main_kernel, depth, planes, names), out_...  68.5 us
    pallas_call x1, Pallas kernels, copied(): pl.pallas_call(copy_kernel, out_shape=tuple((jax.ShapeDtypeStruct(r.shape...  2.57 us

profile of v5, /device:TPU:0, one launch (start us, length us, event | category | flops | bytes accessed | tf_op | source)
XLA Modules:
  0.0 71.9 jit_solution(6200021516879878624)
XLA Ops:
  0.6 68.5 %shard_map.203 = (bf16[2,256,512]{2,1,0:T(8,128)(2,1)}, bf16[2,256,512]{2,1,0:T(8,128)(2,1)}, f32[2,512]{1,0:T(2,128)}, f32[2,384]{1,0:T(2,128)}, f32[2,384]{1,0...) custom-call(bf16[2,256,512]{2,1,0:T(8,128)(2,1)} %refs_0_.1, ...), custom_call_target="tpu_custom_call" | custom-call | tf_op jit(solution)/shard_map/pallas_call | solution.py:938
  69.1 2.6 %shard_map.204 = (bf16[2,256,512]{2,1,0:T(8,128)(2,1)}, bf16[2,256,512]{2,1,0:T(8,128)(2,1)}, f32[2,512]{1,0:T(2,128)}, f32[2,384]{1,0:T(2,128)}, f32[2,384]{1,0...) custom-call(bf16[2,256,512]{2,1,0:T(8,128)(2,1)} %get-tuple-element., ...), custom_call_target="tpu_custom_call" | custom-call | tf_op jit(solution)/shard_map/pallas_call | solution.py:844
